TPU v7x, 256 devices: a whole 4x4x8 slice. The times are simulated.
256 devices in a mesh: ux: 4 (over y_hi, core), uy: 4 (over x), bond: 16 (over y_lo, z).
Axes of the slice: x: 4, y: 4 (y_hi: 2, y_lo: 2; y = y_hi * 2 + y_lo), z: 8, core: 2. Of those that a mesh axis runs over, the one named last changes fastest.
Arguments:
- corner_up: bfloat16 [4, 4, 768, 768], P('ux', 'uy', 'bond'), may hold values from -6 to 6
- edge_top: bfloat16 [4, 4, 768, 4, 768], P('ux', 'uy', 'bond'), may hold values from -0.21875 to 0.21875
- edge_left: bfloat16 [4, 4, 768, 4, 768], P('ux', 'uy', 'bond'), may hold values from -6 to 6
- corner_down: bfloat16 [4, 4, 768, 768], P('ux', 'uy', 'bond'), may hold values from -6 to 6
- edge_bottom: bfloat16 [4, 4, 768, 4, 768], P('ux', 'uy', 'bond'), may hold values from -0.3125 to 0.3125
- site_weights: bfloat16 [4, 4, 4, 4, 4, 4], P('ux', 'uy'), may hold values from -3 to 3
- proj_upper: bfloat16 [4, 4, 768, 4, 768], P('ux', 'uy', 'bond'), may hold values from -0.109375 to 0.109375
- proj_lower: bfloat16 [4, 4, 768, 4, 768], P('ux', 'uy', 'bond'), may hold values from -0.15625 to 0.15625
Outputs:
- new_corner_up: bfloat16 [4, 4, 768, 768], P('ux', 'uy', 'bond')
- new_edge_left: bfloat16 [4, 4, 768, 4, 768], P('ux', 'uy', 'bond')
- new_corner_down: bfloat16 [4, 4, 768, 768], P('ux', 'uy', 'bond')
All inputs are finite; a program needn't handle non-finite values.
Results may differ from a plain program's by a relative error of at most 0.0058.
Values may be sent and summed in bfloat16 or wider, within the bound.
A program may use at most 128 MiB of HBM per device.

v0:
```python
import jax
import jax.numpy as jnp
from jax import lax
from jax.sharding import PartitionSpec as P


def shifted(value, axis, steps):
    count = lax.axis_size(axis)
    pairs = [(source, (source + steps) % count) for source in range(count)]
    return lax.ppermute(value, axis, pairs)


def shards(
    corner_up, edge_top, edge_left, corner_down, edge_bottom, site_weights, proj_upper, proj_lower
):
    corner = corner_up[0, 0]
    top_edge = edge_top[0, 0]
    left_edge = edge_left[0, 0]
    low_corner = corner_down[0, 0]
    bottom_edge = edge_bottom[0, 0]
    weights = site_weights[0, 0]
    upper_proj = proj_upper[0, 0]
    lower_proj = proj_lower[0, 0]
    prev_lower = shifted(lower_proj, "uy", 1)
    stacked = jnp.einsum(
        "alc,lurd->aurdc", left_edge, weights, preferred_element_type=jnp.float32
    ).astype(jnp.bfloat16)
    pieces = lax.all_gather(upper_proj, "bond", axis=0, tiled=True)
    framed_sum = jnp.einsum("aurdc,cdq->aurq", stacked, pieces, preferred_element_type=jnp.float32)
    lowered_sum = jnp.einsum("dc,ckq->dkq", low_corner, pieces, preferred_element_type=jnp.float32)
    framed = framed_sum
    lowered = lowered_sum
    framed = framed.astype(jnp.bfloat16)
    lowered = lowered.astype(jnp.bfloat16)
    new_lower = lax.psum_scatter(
        jnp.einsum("dke,dkq->eq", bottom_edge, lowered, preferred_element_type=jnp.float32),
        "bond",
        scatter_dimension=0,
        tiled=True,
    ).astype(jnp.bfloat16)
    enlarged = jnp.einsum(
        "ab,ekb->ake",
        corner,
        lax.all_gather(top_edge, "bond", axis=0, tiled=True),
        preferred_element_type=jnp.float32,
    ).astype(jnp.bfloat16)
    proj_part = prev_lower
    new_corner = lax.psum_scatter(
        jnp.einsum("akq,ake->qe", proj_part, enlarged, preferred_element_type=jnp.float32),
        "bond",
        scatter_dimension=0,
        tiled=True,
    ).astype(jnp.bfloat16)
    proj_part = prev_lower
    new_edge = lax.psum_scatter(
        jnp.einsum("auq,aurc->qrc", proj_part, framed, preferred_element_type=jnp.float32),
        "bond",
        scatter_dimension=0,
        tiled=True,
    ).astype(jnp.bfloat16)
    moved = shifted((new_corner, new_edge, new_lower), "ux", 1)
    return (moved[0][None, None], moved[1][None, None], moved[2][None, None])


def solution(mesh):
    return jax.shard_map(
        shards,
        mesh=mesh,
        in_specs=(
            P("ux", "uy", "bond", None),
            P("ux", "uy", "bond", None, None),
            P("ux", "uy", "bond", None, None),
            P("ux", "uy", "bond", None),
            P("ux", "uy", "bond", None, None),
            P("ux", "uy", None, None, None, None),
            P("ux", "uy", "bond", None, None),
            P("ux", "uy", "bond", None, None),
        ),
        out_specs=(
            P("ux", "uy", "bond", None),
            P("ux", "uy", "bond", None, None),
            P("ux", "uy", "bond", None),
        ),
        check_vma=False,
    )
```

profile of v0, /device:TPU:1, one launch (start us, length us, event | category | flops | bytes accessed | tf_op | source)
XLA Modules:
  0.0 457.4 jit_solution(3423761415157695681)
XLA Ops:
  8.0 0.7 all-gather.7.cloned.1.call-update
  8.7 1.0 copy.75
  9.7 2.1 collective-permute-start
  11.8 5.7 %collective-permute-done = bf16[48,4,768]{2,0,1:T(8,128)(2,1)S(1)} collective-permute-done((bf16[48,4,768]{2,0,1:T(8,128)(2,1)S(1)}, bf16[48,4,768]{2,0,1:T(8,128)(2,1)S(1)}, u32[]{:S(2)}, u32[]{:S(2)}) %collective-permute-start) | collective-permute-done | bytes 294944 | tf_op jit(solution)/shard_map/ppermute | solution.py:10
  17.5 65.2 %all-gather.5.cloned.1.call-done = bf16[1,1,768,4,768]{4,3,1,0,2:T(4,128)(2,1)} async-done(((bf16[1,1,48,4,768]{4,3,1,0,2:T(4,128)(2,1)}), bf16[1,1,768,4,768]{4,3,1,0,2:T(4,128)(2,1)}) %all-gather.5.cloned.1.call-update) | async-done | bytes 4718608 | tf_op jit(solution)/shard_map/all_gather | solution.py:44
  82.7 4.3 convolution_bitcast_fusion.2
  87.1 2.0 copy.34
  90.4 4.5 fusion.29
  94.9 64.6 %all-gather.7.cloned.1.call-done = bf16[1,1,768,4,768]{4,3,1,0,2:T(4,128)(2,1)} async-done(((bf16[1,1,48,4,768]{4,3,1,0,2:T(4,128)(2,1)}), bf16[1,1,768,4,768]{4,3,1,0,2:T(4,128)(2,1)}) %all-gather.7.cloned.1.call-update) | async-done | bytes 4718608 | tf_op jit(solution)/shard_map/all_gather | solution.py:28
  159.5 3.8 convolution_bitcast_fusion.1
  163.3 2.0 copy.36
  165.3 14.5 %convolution_bitcast_fusion = f32[768,4,768]{0,2,1:T(8,128)} fusion(bf16[768,4,768,1,1]{2,1,0,3,4:T(4,128)(2,1)} %bitcast.70, bf16[48,4,768]{2,0,1:T(8,128)(2,1)S(1)} %collective-permute-done, bf16[4,4,4,48,768]{4,2,3,1,0:T(4,128)(2,1)} %fusion.29), kind=kOutput, calls=%fused_computation.9 | convolution fusion | flops 4530438144 | bytes 19169280 | tf_op jit(solution)/shard_map/auq,aurc->qrc/dot_general | solution.py:56
  179.7 12.1 %copy.19 = f32[768,4,768]{2,1,0:T(4,128)} copy(f32[768,4,768]{0,2,1:T(8,128)} %convolution_bitcast_fusion) | data formatting | bytes 18874368 | tf_op jit(solution)/shard_map/auq,aurc->qrc/dot_general | solution.py:56
  191.8 240.4 %all-reduce.2 = bf16[768,4,768]{2,1,0:T(4,128)(2,1)} all-reduce(f32[768,4,768]{2,1,0:T(4,128)} %copy.19), channel_id=5, replica_groups=mesh['ux'=4,'uy'=4,'bond'=16] {'bond'}, use_global_device_ids=true, to_apply=%region_1.0.clone | all-reduce | flops 2359296 | bytes 14155776
  432.2 1.1 dynamic-slice_convert_fusion
  433.3 9.0 %collective-permute-start.2 = (bf16[48,4,768]{2,0,1:T(8,128)(2,1)S(1)}, bf16[48,4,768]{2,0,1:T(8,128)(2,1)S(1)}, u32[]{:S(2)}, u32[]{:S(2)}) collective-permute-start(bf16[48,4,768]{2,0,1:T(8,128)(2,1)S(1)} %copy.20), channel_id=1, source_target_pairs={{0,64},{64,128},{128,192},{192,0},{1,65},{65,129},{129,193},{193,1... | collective-permute-start | bytes 884744 | tf_op jit(solution)/shard_map/ppermute | solution.py:10
  442.3 1.1 copy.35
  443.5 1.1 copy.37
  444.5 0.9 collective-permute-start.3
  445.9 0.9 copy.23
  446.8 1.2 collective-permute-done.1
  448.0 0.8 copy.22
  448.8 1.3 collective-permute-done.3
  450.2 0.8 copy.24
  (23 shorter events, 2.1 us)
Async XLA Ops:
  7.2 83.2 %copy-start = (bf16[1,1,48,4,768]{4,3,2,1,0:T(4,128)(2,1)S(1)}, bf16[1,1,48,4,768]{4,3,2,1,0:T(4,128)(2,1)}, u32[]{:S(2)}) copy-start(bf16[1,1,48,4,768]{4,3,2,1,0:T(4,128)(2,1)} %param.10) | copy-start | bytes 884740
  7.2 75.5 %all-gather.5.cloned.1.call-start = ((), (), s32[]{:S(2)}) async-start(), calls=%async_computation.2 | async-start | bytes 5013504 | tf_op jit(solution)/shard_map/all_gather | solution.py:44
  7.9 151.6 %all-gather.7.cloned.1.call-start = ((), (), s32[]{:S(2)}) async-start(), calls=%async_computation.3 | async-start | bytes 5013504 | tf_op jit(solution)/shard_map/all_gather | solution.py:28
  8.7 433.6 %reduce-scatter.7.cloned.1.call-start = ((), (), s32[]{:S(2)}) async-start(), calls=%async_computation.4 | async-start | bytes 2506752
  9.7 7.8 %collective-permute-start = (bf16[48,4,768]{2,0,1:T(8,128)(2,1)S(1)}, bf16[48,4,768]{2,0,1:T(8,128)(2,1)S(1)}, u32[]{:S(2)}, u32[]{:S(2)}) collective-permute-start(bf16[48,4,768]{2,0,1:T(8,128)(2,1)S(1)} %bitcast.75), channel_id=1, source_target_pairs={{0,16},{16,32},{32,48},{48,0},{1,17},{17,33},{33,49},{49,1},{2,18}... | collective-permute-start | bytes 884744 | tf_op jit(solution)/shard_map/ppermute | solution.py:10
  87.1 2.1 copy-start.4
  87.1 3.3 copy-start.3
  89.1 70.4 %copy-start.1 = (bf16[1,1,48,4,768]{4,3,2,1,0:T(4,128)(2,1)S(1)}, bf16[1,1,48,4,768]{4,3,2,1,0:T(4,128)(2,1)}, u32[]{:S(2)}) copy-start(bf16[1,1,48,4,768]{4,3,2,1,0:T(4,128)(2,1)} %param.12) | copy-start | bytes 884740
  89.1 70.4 %copy-start.2 = (bf16[1,1,48,768]{3,2,1,0:T(8,128)(2,1)S(1)}, bf16[1,1,48,768]{3,2,1,0:T(8,128)(2,1)}, u32[]{:S(2)}) copy-start(bf16[1,1,48,768]{3,2,1,0:T(8,128)(2,1)} %param.11) | copy-start | bytes 221188
  89.1 354.4 %reduce-scatter.9.cloned.1.call-start = ((), (), s32[]{:S(2)}) async-start(), calls=%async_computation.5 | async-start | bytes 2506752
  433.3 12.6 %collective-permute-start.2 = (bf16[48,4,768]{2,0,1:T(8,128)(2,1)S(1)}, bf16[48,4,768]{2,0,1:T(8,128)(2,1)S(1)}, u32[]{:S(2)}, u32[]{:S(2)}) collective-permute-start(bf16[48,4,768]{2,0,1:T(8,128)(2,1)S(1)} %copy.20), channel_id=1, source_target_pairs={{0,64},{64,128},{128,192},{192,0},{1,65},{65,129},{129,193},{193,1... | collective-permute-start | bytes 884744 | tf_op jit(solution)/shard_map/ppermute | solution.py:10
  443.3 4.7 %collective-permute-start.1 = (bf16[48,768]{0,1:T(8,128)(2,1)S(1)}, bf16[48,768]{0,1:T(8,128)(2,1)S(1)}, u32[]{:S(2)}, u32[]{:S(2)}) collective-permute-start(bf16[48,768]{0,1:T(8,128)(2,1)S(1)} %copy.35), channel_id=1, source_target_pairs={{0,64},{64,128},{128,192},{192,0},{1,65},{65,129},{129,193},{193,1... | collective-permute-start | bytes 221192 | tf_op jit(solution)/shard_map/ppermute | solution.py:10
  444.5 5.6 %collective-permute-start.3 = (bf16[48,768]{0,1:T(8,128)(2,1)S(1)}, bf16[48,768]{0,1:T(8,128)(2,1)S(1)}, u32[]{:S(2)}, u32[]{:S(2)}) collective-permute-start(bf16[48,768]{0,1:T(8,128)(2,1)S(1)} %copy.37), channel_id=1, source_target_pairs={{0,64},{64,128},{128,192},{192,0},{1,65},{65,129},{129,193},{193,1... | collective-permute-start | bytes 221192 | tf_op jit(solution)/shard_map/ppermute | solution.py:10
Sparse Core Ops, SparseCore 0:
  9.8 72.8 all-gather.4
  84.5 74.9 all-gather.6
  162.0 76.2 reduce-scatter.6
  240.7 80.8 reduce-scatter.8
where the time goes:
time: 458 us; the launch traced here: 457 us
  blocking collectives  240 us (52%)
  waiting for transfers between devices  140 us (31%)
  matrix products  27.1 us (6%)
  local copies, waits for them, and re-layouts  23.3 us (5%)
  between operations  14.5 us (3%)
  starting transfers between devices  12.3 us (3%)
    unnamed x1, blocking collectives  240 us
    all_gather x1, waiting for transfers between devices, shards(): lax.all_gather(top_edge, 'bond', axis=0, tiled=True)  65.2 us
    all_gather x1, waiting for transfers between devices, shards(): pieces = lax.all_gather(upper_proj, 'bond', axis=0, tiled=True)  64.6 us
    dot_general x1, matrix products, shards(): jnp.einsum('auq,aurc->qrc', proj_part, framed, preferred_element_type=jnp...  14.5 us
    ppermute x4, starting transfers between devices, shifted(): return lax.ppermute(value, axis, pairs)  12.1 us
    dot_general x1, local copies, waits for them, and re-layouts, shards(): jnp.einsum('auq,aurc->qrc', proj_part, framed, preferred_element_type=jnp...  12.1 us
    unnamed x19, local copies, waits for them, and re-layouts  10.1 us
  transfers between devices with their start and end apart: 8, of which 6 were waited for; matrix products, arithmetic and copies ran while one was open for 11% of the time, Pallas kernels for 0%

commit v1 on v0

v1 whole, which is shorter than its diff:
```python
import jax
import jax.numpy as jnp
import numpy as np
from jax import lax
from jax.experimental import pallas as pl
from jax.experimental.pallas import tpu as pltpu
from jax.sharding import PartitionSpec as P

MESH = pl.DeviceIdType.MESH
BF = jnp.bfloat16
F32 = jnp.float32
ZN = 8
YN = 2
D = 4
CHI = 768
BLK = CHI // (ZN * YN)
HALF = CHI // YN
ROWS = D * BLK
SLABS = 6
COPIES = 96


def mul(a, b, ca=1, cb=0):
    return lax.dot_general(a, b, (((ca,), (cb,)), ((), ())), preferred_element_type=F32)


def kernel(
    pu, pl_, el, et, eb, cu, cd, w, mask, expand,
    out,
    pug, etg, elb, plb, ebb, cub, cdb, mix, xb, fb, lb, ebuf, outp, sbuf, rbuf, fin,
    ssem, rsem, lsem,
):
    bond = lax.axis_index("bond")
    ux = lax.axis_index("ux")
    uy = lax.axis_index("uy")
    yl = lax.div(bond, ZN)
    z = lax.rem(bond, ZN)
    yo = 1 - yl

    def dev(dz=0, other=False, dx=0, dy=0):
        bz = lax.rem(z + (dz + ZN), ZN)
        return (
            lax.rem(ux + (dx + 4), 4),
            lax.rem(uy + (dy + 4), 4),
            (yo if other else yl) * ZN + bz,
        )

    right, left, mate = dev(1), dev(-1), dev(other=True)

    barrier = pltpu.get_barrier_semaphore()
    sources = [left, right, mate, dev(dy=-1), dev(dy=-1, other=True), dev(dx=-1), dev(dx=-1, other=True)]
    for source in sources:
        pl.semaphore_signal(barrier, inc=1, device_id=source, device_id_type=MESH)
    pl.semaphore_wait(barrier, len(sources))

    started = []
    count = [0]

    def rcopy(src, dst, to):
        index = count[0]
        count[0] += 1
        copy = pltpu.make_async_remote_copy(
            src_ref=src, dst_ref=dst, send_sem=ssem.at[index], recv_sem=rsem.at[index],
            device_id=to, device_id_type=MESH,
        )
        copy.start()
        started.append(copy)
        return copy

    def zmod(k):
        return lax.rem(z + (k + ZN), ZN)

    def rows_c(half, zz):
        return pl.ds(pl.multiple_of(half * HALF + zz * BLK, 16), BLK)

    y_pu = rcopy(pu.at[yo], pug.at[:, rows_c(yl, z), :], mate)
    pr = {}
    pr_l = {}
    pr["own", 1] = rcopy(pu.at[yl], pug.at[:, rows_c(yl, z), :], right)
    pr_l["own", 1] = rcopy(pu.at[yl], pug.at[:, rows_c(yl, z), :], left)
    my192 = pl.ds(pl.multiple_of(yl * ROWS, 16), ROWS)
    my48 = pl.ds(pl.multiple_of(yl * BLK, 16), BLK)
    y_el = rcopy(el, elb.at[my192, :], mate)
    x_same = rcopy(pl_, plb.at[my192, :], dev(dy=1))
    x_other = rcopy(pl_, plb.at[my192, :], dev(dy=1, other=True))
    y_cd = rcopy(cd, cdb.at[my48, :], mate)
    y_cu = rcopy(cu, cub.at[my48, :], mate)
    y_eb = rcopy(eb, ebb.at[my192, :], mate)
    local = [
        (pu.at[yl], pug.at[:, rows_c(yl, z), :]),
        (et, etg.at[:, pl.ds(pl.multiple_of(z * BLK, 16), BLK), :]),
        (el, elb.at[my192, :]),
        (eb, ebb.at[my192, :]),
        (cu, cub.at[my48, :]),
        (cd, cdb.at[my48, :]),
    ]
    here = []
    for i, (src, dst) in enumerate(local):
        copy = pltpu.make_async_copy(src, dst, lsem.at[i])
        copy.start()
        here.append(copy)

    spread = mul(expand[...], w[...], 0, 0).astype(BF)
    mix[...] = (mul(spread, expand[...]) * mask[...].astype(F32)).astype(BF)

    def pu_at(half, zz):
        return pug.at[:, rows_c(half, zz), :]

    y_pu.wait_recv()
    pr["oth", 1] = rcopy(pu_at(yo, z), pu_at(yo, z), right)
    pr_l["oth", 1] = rcopy(pu_at(yo, z), pu_at(yo, z), left)

    def forward_pu(m):
        for name, half in (("own", yl), ("oth", yo)):
            if (name, m) in pr:
                pr[name, m].wait_recv()
                if m < 3 or (m == 3 and name == "own"):
                    at = pu_at(half, zmod(-m))
                    pr[name, m + 1] = rcopy(at, at, right)
            if (name, m) in pr_l:
                pr_l[name, m].wait_recv()
                if m < 3 or (m == 3 and name == "oth"):
                    at = pu_at(half, zmod(m))
                    pr_l[name, m + 1] = rcopy(at, at, left)

    er = {}
    er_l = {}

    def et_at(part, zz):
        return etg.at[pl.ds(part * 2, 2), pl.ds(pl.multiple_of(zz * BLK, 16), BLK), :]

    def forward_et(m):
        for part in (0, 1):
            if (part, m) in er:
                er[part, m].wait_recv()
                if m < 3 or (m == 3 and part == 0):
                    at = et_at(part, zmod(-m))
                    er[part, m + 1] = rcopy(at, at, right)
            if (part, m) in er_l:
                er_l[part, m].wait_recv()
                if m < 3 or (m == 3 and part == 1):
                    at = et_at(part, zmod(m))
                    er_l[part, m + 1] = rcopy(at, at, left)

    forward_pu(1)
    forward_pu(2)
    for part in (0, 1):
        er[part, 1] = rcopy(et.at[pl.ds(part * 2, 2)], et_at(part, z), right)
        er_l[part, 1] = rcopy(et.at[pl.ds(part * 2, 2)], et_at(part, z), left)
    forward_pu(3)
    forward_pu(4)

    for copy in here:
        copy.wait()
    y_el.wait_recv()
    y_cd.wait_recv()

    def x_step(d, carry):
        x = mul(elb[...], pug[d]).astype(BF)
        base = pl.multiple_of(d * ROWS, 16)
        xb[0, pl.ds(base, ROWS), :] = x[:ROWS]
        xb[1, pl.ds(base, ROWS), :] = x[ROWS:]
        low = mul(cdb[...], pug[d]).astype(BF)
        base = pl.multiple_of(d * BLK, 16)
        lb[pl.ds(base, BLK), :] = low[:BLK]
        lb[pl.ds(pl.multiple_of(ROWS + d * BLK, 16), BLK), :] = low[BLK:]
        return carry

    lax.fori_loop(0, D, x_step, 0)
    forward_et(1)

    def mix_step(h, carry):
        f = mul(mix[...], xb[h]).astype(BF)
        for r in range(D):
            fb[r, pl.ds(pl.multiple_of(h * ROWS, 16), ROWS), :] = f[r * ROWS:(r + 1) * ROWS]
        return carry

    lax.fori_loop(0, YN, mix_step, 0)
    x_same.wait_recv()
    x_other.wait_recv()
    y_eb.wait_recv()
    y_cu.wait_recv()

    def edge_step(r, carry):
        outp[r] = mul(plb[...], fb[r], 0, 0)
        return carry

    lax.fori_loop(0, D, edge_step, 0)
    outp[4] = mul(ebb[...], lb[...], 0, 0)
    forward_et(2)

    def own(j0, n, h, zz):
        return outp[j0:j0 + n, pl.ds(pl.multiple_of(h * HALF + zz * BLK, 16), BLK), :]

    flows = {}

    def rs_first(j0, n):
        zz = zmod(4)
        for side, h, to in ((0, 0, right), (1, 1, left)):
            sbuf[side, 0, h, j0:j0 + n] = own(j0, n, h, zz).astype(BF)
            flows[j0, side, 1] = rcopy(
                sbuf.at[side, 0, h, pl.ds(j0, n)], rbuf.at[side, 0, h, pl.ds(j0, n)], to
            )

    def rs_next(j0, n, t):
        for side, sign, to in ((0, 1, right), (1, -1, left)):
            flows[j0, side, t - 1].wait_recv()
            zz = zmod(sign * (5 - t))
            for h in range(YN):
                value = own(j0, n, h, zz)
                if t > 2 or h == side:
                    value = value + rbuf[side, t - 2, h, j0:j0 + n].astype(F32)
                sbuf[side, t - 1, h, j0:j0 + n] = value.astype(BF)
            flows[j0, side, t] = rcopy(
                sbuf.at[side, t - 1, :, pl.ds(j0, n)], rbuf.at[side, t - 1, :, pl.ds(j0, n)], to
            )

    outs = []

    def rs_last(j0, n):
        for side in range(2):
            flows[j0, side, 4].wait_recv()
        for h in range(YN):
            value = own(j0, n, h, z)
            for side in range(2):
                value = value + rbuf[side, 3, h, j0:j0 + n].astype(F32)
            fin[h, j0:j0 + n] = value.astype(BF)
        outs.append(rcopy(fin.at[yl, pl.ds(j0, n)], out.at[yl, pl.ds(j0, n)], dev(dx=1)))
        outs.append(rcopy(fin.at[yo, pl.ds(j0, n)], out.at[yl, pl.ds(j0, n)], dev(dx=1, other=True)))

    waves = [(0, 2), (2, 2), (4, 1)]
    for j0, n in waves:
        rs_first(j0, n)
    forward_et(3)
    for j0, n in waves:
        rs_next(j0, n, 2)
    forward_et(4)

    def corner_step(k, carry):
        part = mul(cub[...], etg[k], 1, 1).astype(BF)
        ebuf[pl.ds(pl.multiple_of(k * BLK, 16), BLK), :] = part[:BLK]
        ebuf[pl.ds(pl.multiple_of(ROWS + k * BLK, 16), BLK), :] = part[BLK:]
        return carry

    lax.fori_loop(0, D, corner_step, 0)
    outp[5] = mul(plb[...], ebuf[...], 0, 0)
    rs_first(5, 1)
    for j0, n in waves:
        rs_next(j0, n, 3)
    rs_next(5, 1, 2)
    for j0, n in waves:
        rs_next(j0, n, 4)
    rs_next(5, 1, 3)
    rs_next(5, 1, 4)
    for j0, n in waves:
        rs_last(j0, n)
    rs_last(5, 1)
    for copy in outs:
        copy.wait_recv()
    for copy in started:
        copy.wait_send()


def constants():
    index = np.arange(D * D * BLK)
    mask = (index[:, None] % BLK == index[None, :] % BLK).astype(np.float32)
    expand = (np.arange(D * D)[:, None] == index[None, :] // BLK).astype(np.float32)
    return jnp.asarray(mask, BF), jnp.asarray(expand, BF)


def shards(
    corner_up, edge_top, edge_left, corner_down, edge_bottom, site_weights, proj_upper, proj_lower
):
    def rows(t):
        return t[0, 0].transpose(1, 0, 2)

    pu = proj_upper[0, 0].reshape(BLK, D, YN, HALF).transpose(2, 1, 0, 3)
    low = rows(proj_lower).reshape(ROWS, CHI)
    el = rows(edge_left).reshape(ROWS, CHI)
    et = rows(edge_top)
    eb = rows(edge_bottom).reshape(ROWS, CHI)
    w = site_weights[0, 0].transpose(2, 1, 3, 0).reshape(D * D, D * D)
    mask, expand = constants()
    vmem = pl.BlockSpec(memory_space=pltpu.VMEM)
    rows2 = YN * ROWS
    out = pl.pallas_call(
        kernel,
        out_shape=jax.ShapeDtypeStruct((YN, SLABS, BLK, HALF), BF),
        in_specs=[vmem] * 10,
        out_specs=vmem,
        scratch_shapes=[
            pltpu.VMEM((D, CHI, HALF), BF),
            pltpu.VMEM((D, HALF, CHI), BF),
            pltpu.VMEM((rows2, CHI), BF),
            pltpu.VMEM((rows2, CHI), BF),
            pltpu.VMEM((rows2, CHI), BF),
            pltpu.VMEM((YN * BLK, CHI), BF),
            pltpu.VMEM((YN * BLK, CHI), BF),
            pltpu.VMEM((D * ROWS, D * ROWS), BF),
            pltpu.VMEM((YN, D * ROWS, HALF), BF),
            pltpu.VMEM((D, rows2, HALF), BF),
            pltpu.VMEM((rows2, HALF), BF),
            pltpu.VMEM((rows2, HALF), BF),
            pltpu.VMEM((SLABS, CHI, HALF), F32),
            pltpu.VMEM((2, 4, YN, SLABS, BLK, HALF), BF),
            pltpu.VMEM((2, 4, YN, SLABS, BLK, HALF), BF),
            pltpu.VMEM((YN, SLABS, BLK, HALF), BF),
            pltpu.SemaphoreType.DMA((COPIES,)),
            pltpu.SemaphoreType.DMA((COPIES,)),
            pltpu.SemaphoreType.DMA((8,)),
        ],
        compiler_params=pltpu.CompilerParams(
            collective_id=0, has_side_effects=True, vmem_limit_bytes=56 * 1024 * 1024
        ),
    )(pu, low, el, et, eb, corner_up[0, 0], corner_down[0, 0], w, mask, expand)
    edge = out[:, :D].transpose(2, 1, 0, 3).reshape(1, 1, BLK, D, CHI)
    lower = out[:, D].transpose(1, 0, 2).reshape(1, 1, BLK, CHI)
    upper = out[:, D + 1].transpose(1, 0, 2).reshape(1, 1, BLK, CHI)
    return upper, edge, lower


def solution(mesh):
    return jax.shard_map(
        shards,
        mesh=mesh,
        in_specs=(
            P("ux", "uy", "bond", None),
            P("ux", "uy", "bond", None, None),
            P("ux", "uy", "bond", None, None),
            P("ux", "uy", "bond", None),
            P("ux", "uy", "bond", None, None),
            P("ux", "uy", None, None, None, None),
            P("ux", "uy", "bond", None, None),
            P("ux", "uy", "bond", None, None),
        ),
        out_specs=(
            P("ux", "uy", "bond", None),
            P("ux", "uy", "bond", None, None),
            P("ux", "uy", "bond", None),
        ),
        check_vma=False,
    )
```

time: 458 us -> 116 us (0.25)
  blocking collectives: 240 us -> 0 us
  waiting for transfers between devices: 140 us -> 0 us
  Pallas kernels: 0 us -> 103 us
  matrix products: 27.1 us -> 0 us
  between operations: 14.5 us -> 0.69 us
  starting transfers between devices: 12.3 us -> 0 us
  local copies, waits for them, and re-layouts: 23.3 us -> 12.1 us
    unnamed x1 -> x0, blocking collectives: 240 us -> none
    all_gather x2 -> x0, waiting for transfers between devices: 130 us -> none  [the longest x1 65.2 us: shards(): lax.all_gather(top_edge, 'bond', axis=0, tiled=True)]
    pallas_call x0 -> x1, Pallas kernels: none -> 103 us  [shards(): pl.pallas_call(kernel, out_shape=jax.ShapeDtypeStruct((YN, SLABS, BLK, HA...]
    dot_general x4 -> x0, matrix products: 27.1 us -> none  [the longest x1 14.5 us: shards(): jnp.einsum('auq,aurc->qrc', proj_part, framed, preferred_element_type=jnp...]
    ppermute x4 -> x0, starting transfers between devices: 12.1 us -> none  [shifted(): return lax.ppermute(value, axis, pairs)]
    dot_general x1 -> x0, local copies, waits for them, and re-layouts: 12.1 us -> none  [shards(): jnp.einsum('auq,aurc->qrc', proj_part, framed, preferred_element_type=jnp...]
    ppermute x4 -> x0, waiting for transfers between devices: 8.74 us -> none  [shifted(): return lax.ppermute(value, axis, pairs)]
    unnamed x19 -> x9, local copies, waits for them, and re-layouts: 10.1 us -> 2.92 us
  transfers between devices with their start and end apart: 8 -> 0, of which waited for: 6 -> 0; matrix products, arithmetic and copies ran while one was open for 11% -> 0% of each run, Pallas kernels for 0% -> 0%
where the time goes in v1:
time: 116 us
  Pallas kernels  103 us (89%)
  local copies, waits for them, and re-layouts  12.1 us (10%)
    pallas_call x1, Pallas kernels, shards(): pl.pallas_call(kernel, out_shape=jax.ShapeDtypeStruct((YN, SLABS, BLK, HA...  103 us
    transpose x3, local copies, waits for them, and re-layouts, rows(): return t[0, 0].transpose(1, 0, 2)  3.23 us
    unnamed x9, local copies, waits for them, and re-layouts  2.92 us

profile of v1, /device:TPU:1, one launch (start us, length us, event | category | flops | bytes accessed | tf_op | source)
XLA Modules:
  0.0 116.2 jit_solution(9991067085501315875)
XLA Ops:
  0.6 0.0 copy-start.1
  0.6 0.0 copy-start
  0.7 1.0 copy.24
  1.6 0.7 reshape.30.w
  2.3 1.7 %copy.36 = bf16[1,1,48,4,768]{4,2,3,1,0:T(8,128)(2,1)} copy(bf16[1,1,48,4,768]{4,3,2,1,0:T(4,128)(2,1)} %param.11) | data formatting | bytes 589824 | tf_op args[1]
  4.0 0.0 copy-start.2
  4.0 1.7 %copy.21 = bf16[4,48,768]{2,1,0:T(8,128)(2,1)} copy(bf16[4,48,768]{2,0,1:T(4,128)(2,1)} %bitcast.40) | data formatting | bytes 589824 | tf_op jit(solution)/shard_map/transpose | solution.py:275
  5.8 0.0 copy-done
  5.8 0.8 copy.23
  6.5 0.0 copy-done.1
  6.5 0.1 reshape.34
  6.6 0.7 copy.35
  7.4 0.0 copy-done.2
  7.4 0.7 copy.20
  8.1 103.4 %shard_map.121 = bf16[2,6,48,384]{3,2,1,0:T(8,128)(2,1)} custom-call(bf16[2,4,48,384]{3,2,1,0:T(8,128)(2,1)} %bitcast.38, bf16[192,768]{1,0:T(8,128)(2,1)} %bitcast.39, bf16[192,768]{1,0:T(8,128)(2,1)} %bitcast.36, bf16[4,48,768]{2,1,0:T(8,128)(2,1)} %bitcast.35, bf16[192,768]{1,0:T(8,128)(2,1)} %bitcast.37, bf16[48,768]{1,0:T(8,128)(2,1)} %bitcast.43, ...), custom_call_target="tpu_custom_call" | custom-call | tf_op jit(solution)/shard_map/pallas_call | solution.py:286
  111.5 0.9 slice_bitcast_fusion.1
  112.5 1.0 slice_bitcast_fusion
  113.5 0.3 copy.31
  113.8 0.9 reshape.35
  114.7 0.1 copy.27
  114.7 0.7 reshape.33
  115.4 0.1 copy.25
  115.5 0.7 reshape.31
Async XLA Ops:
  0.6 5.9 %copy-start.1 = (bf16[1,1,48,4,768]{4,3,2,1,0:T(4,128)(2,1)S(1)}, bf16[1,1,48,4,768]{4,3,2,1,0:T(4,128)(2,1)}, u32[]{:S(2)}) copy-start(bf16[1,1,48,4,768]{4,3,2,1,0:T(4,128)(2,1)} %param.16) | copy-start | bytes 884740
  0.6 5.1 %copy-start = (bf16[1,1,48,4,768]{4,3,2,1,0:T(4,128)(2,1)S(1)}, bf16[1,1,48,4,768]{4,3,2,1,0:T(4,128)(2,1)}, u32[]{:S(2)}) copy-start(bf16[1,1,48,4,768]{4,3,2,1,0:T(4,128)(2,1)} %param.14) | copy-start | bytes 884740
  4.0 3.4 %copy-start.2 = (bf16[1,1,48,4,768]{4,3,2,1,0:T(4,128)(2,1)S(1)}, bf16[1,1,48,4,768]{4,3,2,1,0:T(4,128)(2,1)}, u32[]{:S(2)}) copy-start(bf16[1,1,48,4,768]{4,3,2,1,0:T(4,128)(2,1)} %param.17) | copy-start | bytes 884740

commit v2 on v1

v2 whole, which is shorter than its diff:
```python
import jax
import jax.numpy as jnp
from jax import lax
from jax.experimental import pallas as pl
from jax.experimental.pallas import tpu as pltpu
from jax.sharding import PartitionSpec as P

MESH = pl.DeviceIdType.MESH
BF = jnp.bfloat16
F32 = jnp.float32
ZN = 8
YN = 2
D = 4
CHI = 768
BLK = CHI // (ZN * YN)
HALF = CHI // YN
ROWS = D * BLK
SLABS = 6
COPIES = 96


def mul(a, b, ca=1, cb=0):
    return lax.dot_general(a, b, (((ca,), (cb,)), ((), ())), preferred_element_type=F32)


def kernel(
    pu, low, el, et, eb, cu, cd, w,
    out,
    put, pug, cug, etb, elb, plb, lpb, ebb, cdb, mix, xb, fb, lb, pick, e2, er, ebuf, outp, sbuf, rbuf, fin,
    ssem, rsem, asem, bsem, lsem,
):
    bond = lax.axis_index("bond")
    ux = lax.axis_index("ux")
    uy = lax.axis_index("uy")
    yl = lax.div(bond, ZN)
    z = lax.rem(bond, ZN)
    yo = 1 - yl
    zh = lax.div(z, ZN // 2)
    zq = lax.rem(z, ZN // 2)

    def zmod(k):
        return lax.rem(z + (k + ZN), ZN)

    def at_bond(half, zz, dx=0, dy=0):
        return (lax.rem(ux + (dx + 4), 4), lax.rem(uy + (dy + 4), 4), half * ZN + zz)

    right, left, mate = at_bond(yl, zmod(1)), at_bond(yl, zmod(-1)), at_bond(yo, z)

    barrier = pltpu.get_barrier_semaphore()
    sources = [
        left, right, mate,
        at_bond(yl, z, dy=-1), at_bond(yo, z, dy=-1), at_bond(yl, z, dx=-1), at_bond(yo, z, dx=-1),
    ]

    def greet(to):
        pl.semaphore_signal(barrier, inc=1, device_id=to, device_id_type=MESH)

    for source in sources:
        greet(source)
    for half in range(YN):
        for q in range(ZN // 2):
            zz = yl * (ZN // 2) + q

            @pl.when(half * ZN + zz != bond)
            def _():
                greet(at_bond(half, zz))

    turned = jnp.transpose(pu[...], (1, 0, 2))
    put[0] = turned[:, :, :HALF]
    put[1] = turned[:, :, HALF:]
    pl.semaphore_wait(barrier, len(sources) + ZN - jnp.where(zh == yl, 1, 0))

    started = []
    count = [0]

    def rcopy(src, dst, to):
        index = count[0]
        count[0] += 1
        copy = pltpu.make_async_remote_copy(
            src_ref=src, dst_ref=dst, send_sem=ssem.at[index], recv_sem=rsem.at[index],
            device_id=to, device_id_type=MESH,
        )
        copy.start()
        started.append(copy)
        return copy

    def rows_c(half, zz):
        return pl.ds(pl.multiple_of(half * HALF + zz * BLK, 16), BLK)

    def rows_z(zz):
        return pl.ds(pl.multiple_of(zz * BLK, 16), BLK)

    my192 = pl.ds(pl.multiple_of(yl * ROWS, 16), ROWS)
    my48 = pl.ds(pl.multiple_of(yl * BLK, 16), BLK)

    def pu_at(half, zz):
        return pug.at[:, rows_c(half, zz), :]

    def cu_at(zz, part=None):
        if part is None:
            return cug.at[rows_z(zz), :]
        return cug.at[rows_z(zz), pl.ds(part * HALF, HALF)]

    pr, ql = {}, {}
    pr["own", 1] = rcopy(put.at[yl], pu_at(yl, z), right)
    ql["own", 1] = rcopy(put.at[yl], pu_at(yl, z), left)
    y_pu = rcopy(put.at[yo], pu_at(yl, z), mate)
    pr["cu", 1] = rcopy(cu, cu_at(z), right)
    ql["cu", 1] = rcopy(cu, cu_at(z), left)
    here = []
    for i, (src, dst) in enumerate([(put.at[yl], pu_at(yl, z)), (cu, cu_at(z)), (cd, cdb.at[my48, :])]):
        copy = pltpu.make_async_copy(src, dst, lsem.at[i])
        copy.start()
        here.append(copy)
    etb[:, yl] = jnp.transpose(et[...], (1, 0, 2))
    y_et = rcopy(etb.at[:, yl], etb.at[:, yl], mate)
    plb[my192, :] = jnp.transpose(low[...], (1, 0, 2)).reshape(ROWS, CHI)
    x_same = rcopy(plb.at[my192, :], lpb.at[my192, :], at_bond(yl, z, dy=1))
    x_other = rcopy(plb.at[my192, :], lpb.at[my192, :], at_bond(yo, z, dy=1))
    y_pu.wait_recv()
    pr["oth", 1] = rcopy(pu_at(yo, z), pu_at(yo, z), right)
    ql["oth", 1] = rcopy(pu_at(yo, z), pu_at(yo, z), left)
    elb[my192, :] = jnp.transpose(el[...], (1, 0, 2)).reshape(ROWS, CHI)
    y_el = rcopy(elb.at[my192, :], elb.at[my192, :], mate)
    y_cd = rcopy(cd, cdb.at[my48, :], mate)
    ebb[my192, :] = jnp.transpose(eb[...], (1, 0, 2)).reshape(ROWS, CHI)
    y_eb = rcopy(ebb.at[my192, :], ebb.at[my192, :], mate)

    def forward(name, m):
        for flow, sign, to, last in ((pr, -1, right, "own"), (ql, 1, left, "oth")):
            if (name, m) not in flow:
                continue
            flow[name, m].wait_recv()
            zz = zmod(sign * m)
            if name == "cu":
                if m < 4:
                    at = cu_at(zz) if m < 3 else cu_at(zz, 0 if last == "own" else 1)
                    flow[name, m + 1] = rcopy(at, at, to)
            elif m < 3 or (m == 3 and name == last):
                at = pu_at(yl if name == "own" else yo, zz)
                flow[name, m + 1] = rcopy(at, at, to)

    forward("own", 1)
    forward("cu", 1)
    size = D * D * BLK
    rowi = lax.broadcasted_iota(jnp.int32, (size, D ** 3), 0)
    coli = lax.broadcasted_iota(jnp.int32, (size, D ** 3), 1)
    legs = lax.rem(lax.div(rowi, BLK), D) * D + lax.div(rowi, ROWS)
    weights = w[...].reshape(D ** 3, D)
    spread = jnp.zeros((size, D * D), F32)
    for l in range(D):
        one = jnp.where(coli == legs + l * D * D, 1.0, 0.0).astype(BF)
        d_at = lax.broadcasted_iota(jnp.int32, (D, D * D), 0) * D + l
        col = lax.broadcasted_iota(jnp.int32, (D, D * D), 1)
        spread = spread + mul(mul(one, weights).astype(BF), jnp.where(col == d_at, 1.0, 0.0).astype(BF))
    leg = lax.broadcasted_iota(jnp.int32, (D * D, size), 0)
    pos = lax.broadcasted_iota(jnp.int32, (D * D, size), 1)
    expand = jnp.where(leg == lax.div(pos, BLK), 1.0, 0.0).astype(BF)
    full = mul(spread.astype(BF), expand)
    inrow = lax.rem(lax.broadcasted_iota(jnp.int32, (size, 1), 0), BLK)
    incol = lax.rem(lax.broadcasted_iota(jnp.int32, (1, size), 1), BLK)
    mix[...] = jnp.where(inrow == incol, full, 0.0).astype(BF)

    forward("oth", 1)
    forward("cu", 2)
    forward("own", 2)
    forward("oth", 2)
    lane = lax.broadcasted_iota(jnp.int32, (1, HALF), 1)
    upper = jnp.where(lane >= ROWS, 1, 0)
    rest = lane - upper * ROWS
    target = 3 * 2 * BLK + upper * BLK + rest + lax.div(rest, BLK) * (HALF - BLK)
    pick[...] = jnp.where(
        lax.broadcasted_iota(jnp.int32, pick.shape, 0) == target, 1.0, 0.0
    ).astype(BF)

    forward("cu", 3)
    forward("own", 3)
    forward("oth", 3)
    for copy in here:
        copy.wait()
    y_et.wait_recv()
    forward("cu", 4)
    e2[...] = mul(cug[...], etb[...].reshape(HALF, CHI), 1, 1).astype(BF).reshape(ZN, BLK, HALF)

    def er_at(half, q):
        return er.at[half, :, pl.ds(pl.multiple_of(q * HALF, 128), HALF)]

    slot = yl * (ZN // 2) + zq

    def exchange(dz):
        return pltpu.make_async_remote_copy(
            src_ref=e2.at[zmod(dz)], dst_ref=er_at(yl, zq), send_sem=asem.at[dz], recv_sem=bsem.at[slot],
            device_id=at_bond(zh, zmod(dz)), device_id_type=MESH,
        )

    for dz in (4, 3, 5, 2, 6, 1, 7):
        exchange(dz).start()

    @pl.when(zh == yl)
    def _():
        pltpu.make_async_copy(e2.at[z], er_at(yl, zq), bsem.at[slot]).start()

    @pl.when(zh != yl)
    def _():
        exchange(0).start()

    forward("own", 4)
    forward("oth", 4)
    y_el.wait_recv()
    y_cd.wait_recv()

    def x_step(d, carry):
        x = mul(elb[...], pug[d]).astype(BF)
        base = pl.multiple_of(d * ROWS, 16)
        xb[0, pl.ds(base, ROWS), :] = x[:ROWS]
        xb[1, pl.ds(base, ROWS), :] = x[ROWS:]
        return carry

    lax.fori_loop(0, D, x_step, 0)

    def mix_step(h, carry):
        f = mul(mix[...], xb[h]).astype(BF)
        for r in range(D):
            fb[r, pl.ds(pl.multiple_of(h * ROWS, 16), ROWS), :] = f[r * ROWS:(r + 1) * ROWS]
        return carry

    lax.fori_loop(0, YN, mix_step, 0)
    x_same.wait_recv()
    x_other.wait_recv()

    def edge_step(r, carry):
        outp[r] = mul(lpb[...], fb[r], 0, 0)
        return carry

    def own(j0, n, h, zz):
        return outp[j0:j0 + n, pl.ds(pl.multiple_of(h * HALF + zz * BLK, 16), BLK), :]

    flows = {}

    def rs_first(j0, n):
        zz = zmod(4)
        for side, h, to in ((0, 0, right), (1, 1, left)):
            sbuf[side, 0, h, j0:j0 + n] = own(j0, n, h, zz).astype(BF)
            flows[j0, side, 1] = rcopy(
                sbuf.at[side, 0, h, pl.ds(j0, n)], rbuf.at[side, 0, h, pl.ds(j0, n)], to
            )

    def rs_next(j0, n, t):
        for side, sign, to in ((0, 1, right), (1, -1, left)):
            flows[j0, side, t - 1].wait_recv()
            zz = zmod(sign * (5 - t))
            for h in range(YN):
                value = own(j0, n, h, zz)
                if t > 2 or h == side:
                    value = value + rbuf[side, t - 2, h, j0:j0 + n].astype(F32)
                sbuf[side, t - 1, h, j0:j0 + n] = value.astype(BF)
            flows[j0, side, t] = rcopy(
                sbuf.at[side, t - 1, :, pl.ds(j0, n)], rbuf.at[side, t - 1, :, pl.ds(j0, n)], to
            )

    outs = []

    def rs_last(j0, n):
        for side in range(2):
            flows[j0, side, 4].wait_recv()
        for h in range(YN):
            value = own(j0, n, h, z)
            for side in range(2):
                value = value + rbuf[side, 3, h, j0:j0 + n].astype(F32)
            fin[h, j0:j0 + n] = value.astype(BF)
        outs.append(rcopy(fin.at[yl, pl.ds(j0, n)], out.at[yl, pl.ds(j0, n)], at_bond(yl, z, dx=1)))
        outs.append(rcopy(fin.at[yo, pl.ds(j0, n)], out.at[yl, pl.ds(j0, n)], at_bond(yo, z, dx=1)))

    waves = [(0, 2), (2, 2), (4, 1), (5, 1)]
    lax.fori_loop(0, 2, edge_step, 0)
    rs_first(0, 2)
    lax.fori_loop(2, 4, edge_step, 0)
    rs_first(2, 2)

    def low_step(d, carry):
        part = mul(cdb[...], pug[d]).astype(BF)
        lb[pl.ds(pl.multiple_of(d * BLK, 16), BLK), :] = part[:BLK]
        lb[pl.ds(pl.multiple_of(ROWS + d * BLK, 16), BLK), :] = part[BLK:]
        return carry

    lax.fori_loop(0, D, low_step, 0)
    y_eb.wait_recv()
    outp[4] = mul(ebb[...], lb[...], 0, 0)
    rs_first(4, 1)
    rs_next(0, 2, 2)
    for half in range(YN):
        for q in range(ZN // 2):
            pltpu.make_async_copy(e2.at[0], er_at(half, q), bsem.at[half * (ZN // 2) + q]).wait()

    def pick_step(k, carry):
        shift = pl.multiple_of((3 - k) * 2 * BLK, 16)
        part = mul(er[...].reshape(YN * BLK, 4 * HALF), pick[pl.ds(shift, 4 * HALF), :]).astype(BF)
        ebuf[pl.ds(pl.multiple_of(k * BLK, 16), BLK), :] = part[:BLK]
        ebuf[pl.ds(pl.multiple_of(ROWS + k * BLK, 16), BLK), :] = part[BLK:]
        return carry

    lax.fori_loop(0, D, pick_step, 0)
    outp[5] = mul(lpb[...], ebuf[...], 0, 0)
    rs_first(5, 1)
    for j0, n in waves[1:]:
        rs_next(j0, n, 2)
    for t in (3, 4):
        for j0, n in waves:
            rs_next(j0, n, t)
    for j0, n in waves:
        rs_last(j0, n)
    for copy in outs:
        copy.wait_recv()
    for copy in started:
        copy.wait_send()
    for dz in range(1, ZN):
        exchange(dz).wait_send()

    @pl.when(zh != yl)
    def _():
        exchange(0).wait_send()


def arrange(parts, edge, lower, upper):
    halves = [parts[0, :D], parts[1, :D]]
    edge[...] = jnp.transpose(jnp.concatenate(halves, axis=2), (1, 0, 2))
    lower[:, :HALF] = parts[0, D]
    lower[:, HALF:] = parts[1, D]
    first, second = parts[0, D + 1], parts[1, D + 1]
    upper[...] = jnp.concatenate(
        [first[:, :ROWS], second[:, :ROWS], first[:, ROWS:], second[:, ROWS:]], axis=1
    )


def shards(
    corner_up, edge_top, edge_left, corner_down, edge_bottom, site_weights, proj_upper, proj_lower
):
    vmem = pl.BlockSpec(memory_space=pltpu.VMEM)
    rows2 = YN * ROWS
    size = D * ROWS
    parts = pl.pallas_call(
        kernel,
        out_shape=jax.ShapeDtypeStruct((YN, SLABS, BLK, HALF), BF),
        in_specs=[vmem] * 8,
        out_specs=vmem,
        scratch_shapes=[
            pltpu.VMEM((YN, D, BLK, HALF), BF),
            pltpu.VMEM((D, CHI, HALF), BF),
            pltpu.VMEM((HALF, CHI), BF),
            pltpu.VMEM((D, YN, BLK, CHI), BF),
            pltpu.VMEM((rows2, CHI), BF),
            pltpu.VMEM((rows2, CHI), BF),
            pltpu.VMEM((rows2, CHI), BF),
            pltpu.VMEM((rows2, CHI), BF),
            pltpu.VMEM((YN * BLK, CHI), BF),
            pltpu.VMEM((size, size), BF),
            pltpu.VMEM((YN, size, HALF), BF),
            pltpu.VMEM((D, rows2, HALF), BF),
            pltpu.VMEM((rows2, HALF), BF),
            pltpu.VMEM((4 * HALF + 6 * BLK, HALF), BF),
            pltpu.VMEM((ZN, BLK, HALF), BF),
            pltpu.VMEM((YN, BLK, 4 * HALF), BF),
            pltpu.VMEM((rows2, HALF), BF),
            pltpu.VMEM((SLABS, CHI, HALF), F32),
            pltpu.VMEM((2, 4, YN, SLABS, BLK, HALF), BF),
            pltpu.VMEM((2, 4, YN, SLABS, BLK, HALF), BF),
            pltpu.VMEM((YN, SLABS, BLK, HALF), BF),
            pltpu.SemaphoreType.DMA((COPIES,)),
            pltpu.SemaphoreType.DMA((COPIES,)),
            pltpu.SemaphoreType.DMA((ZN,)),
            pltpu.SemaphoreType.DMA((ZN,)),
            pltpu.SemaphoreType.DMA((8,)),
        ],
        compiler_params=pltpu.CompilerParams(
            collective_id=0, has_side_effects=True, vmem_limit_bytes=56 * 1024 * 1024
        ),
    )(
        proj_upper[0, 0], proj_lower[0, 0], edge_left[0, 0], edge_top[0, 0], edge_bottom[0, 0],
        corner_up[0, 0], corner_down[0, 0], site_weights[0, 0],
    )
    edge, lower, upper = pl.pallas_call(
        arrange,
        out_shape=(
            jax.ShapeDtypeStruct((BLK, D, CHI), BF),
            jax.ShapeDtypeStruct((BLK, CHI), BF),
            jax.ShapeDtypeStruct((BLK, CHI), BF),
        ),
        in_specs=[vmem],
        out_specs=(vmem, vmem, vmem),
    )(parts)
    return upper[None, None], edge[None, None], lower[None, None]


def solution(mesh):
    return jax.shard_map(
        shards,
        mesh=mesh,
        in_specs=(
            P("ux", "uy", "bond", None),
            P("ux", "uy", "bond", None, None),
            P("ux", "uy", "bond", None, None),
            P("ux", "uy", "bond", None),
            P("ux", "uy", "bond", None, None),
            P("ux", "uy", None, None, None, None),
            P("ux", "uy", "bond", None, None),
            P("ux", "uy", "bond", None, None),
        ),
        out_specs=(
            P("ux", "uy", "bond", None),
            P("ux", "uy", "bond", None, None),
            P("ux", "uy", "bond", None),
        ),
        check_vma=False,
    )
```

time: 116 us -> 91 us (0.78)
  Pallas kernels: 103 us -> 90.2 us
  local copies, waits for them, and re-layouts: 12.1 us -> 0 us
    pallas_call x1, Pallas kernels: 103 us -> 88.3 us  [shards(): pl.pallas_call(kernel, out_shape=jax.ShapeDtypeStruct((YN, SLABS, BLK, HA...]
    transpose x8 -> x0, local copies, waits for them, and re-layouts: 6.28 us -> none  [the longest x3 3.23 us: rows(): return t[0, 0].transpose(1, 0, 2)]
    unnamed x9 -> x0, local copies, waits for them, and re-layouts: 2.92 us -> none
    reshape x3 -> x0, local copies, waits for them, and re-layouts: 2.05 us -> none  [the longest x1 0.68 us: shards(): w = site_weights[0, 0].transpose(2, 1, 3, 0).reshape(D * D, D * D)]
    pallas_call x0 -> x1, Pallas kernels: none -> 1.89 us  [shards(): pl.pallas_call(arrange, out_shape=(jax.ShapeDtypeStruct((BLK, D, CHI), BF...]
where the time goes in v2:
time: 91 us; the launch traced here: 90.8 us
  Pallas kernels  90.2 us (99%)
    pallas_call x1, Pallas kernels, shards(): pl.pallas_call(kernel, out_shape=jax.ShapeDtypeStruct((YN, SLABS, BLK, HA...  88.3 us
    pallas_call x1, Pallas kernels, shards(): pl.pallas_call(arrange, out_shape=(jax.ShapeDtypeStruct((BLK, D, CHI), BF...  1.89 us

profile of v2, /device:TPU:1, one launch (start us, length us, event | category | flops | bytes accessed | tf_op | source)
XLA Modules:
  0.0 90.8 jit_solution(13826217334566821907)
XLA Ops:
  0.6 88.3 %shard_map.103.parts = bf16[2,6,48,384]{3,2,1,0:T(8,128)(2,1)} custom-call(bf16[48,4,768]{2,1,0:T(4,128)(2,1)} %bitcast.11, bf16[48,4,768]{2,1,0:T(4,128)(2,1)} %bitcast.12, bf16[48,4,768]{2,1,0:T(4,128)(2,1)} %bitcast.13, bf16[48,4,768]{2,1,0:T(4,128)(2,1)} %bitcast.14, bf16[48,4,768]{2,1,0:T(4,128)(2,1)} %bitcast.15, bf16[48,768]{1,0:T(8,128)(2,1)} %bitcast.16, ...), custom_call_target="tpu_custom_call" | custom-call | tf_op jit(solution)/shard_map/pallas_call | solution.py:341
  88.9 1.9 %shard_map.104 = (bf16[48,4,768]{2,1,0:T(4,128)(2,1)}, bf16[48,768]{1,0:T(8,128)(2,1)}, bf16[48,768]{1,0:T(8,128)(2,1)}) custom-call(bf16[2,6,48,384]{3,2,1,0:T(8,128)(2,1)} %shard_map.103.parts), custom_call_target="tpu_custom_call" | custom-call | tf_op jit(solution)/shard_map/pallas_call | solution.py:381

commit v3 on v2

--- a/solution.py
+++ b/solution.py
@@ -24,9 +24,9 @@
 
 
 def kernel(
-    pu, low, el, et, eb, cu, cd, w,
-    out,
-    put, pug, cug, etb, elb, plb, lpb, ebb, cdb, mix, xb, fb, lb, pick, e2, er, ebuf, outp, sbuf, rbuf, fin,
+    pu_in, low_in, el_in, et_in, eb_in, cu_in, cd_in, w_in,
+    edge_out, lower_out, upper_out,
+    pu, low, el, et, eb, w, put, pug, cug, etb, elb, plb, lpb, ebb, cdb, mix, xb, fb, lb, pick, e2, er, ebuf, outp, sbuf, rbuf, fin, fin_edge,
     ssem, rsem, asem, bsem, lsem,
 ):
     bond = lax.axis_index("bond")
@@ -46,6 +46,16 @@
 
     right, left, mate = at_bond(yl, zmod(1)), at_bond(yl, zmod(-1)), at_bond(yo, z)
 
+    my48 = pl.ds(pl.multiple_of(yl * BLK, 16), BLK)
+    loads = []
+    for i, (src, dst) in enumerate([
+        (pu_in, pu), (cu_in, cug.at[pl.ds(pl.multiple_of(z * BLK, 16), BLK), :]), (et_in, et), (low_in, low),
+        (el_in, el), (eb_in, eb), (cd_in, cdb.at[my48, :]), (w_in, w),
+    ]):
+        load = pltpu.make_async_copy(src, dst, lsem.at[i])
+        load.start()
+        loads.append(load)
+
     barrier = pltpu.get_barrier_semaphore()
     sources = [
         left, right, mate,
@@ -65,6 +75,7 @@
             def _():
                 greet(at_bond(half, zz))
 
+    loads[0].wait()
     turned = jnp.transpose(pu[...], (1, 0, 2))
     put[0] = turned[:, :, :HALF]
     put[1] = turned[:, :, HALF:]
@@ -91,7 +102,6 @@
         return pl.ds(pl.multiple_of(zz * BLK, 16), BLK)
 
     my192 = pl.ds(pl.multiple_of(yl * ROWS, 16), ROWS)
-    my48 = pl.ds(pl.multiple_of(yl * BLK, 16), BLK)
 
     def pu_at(half, zz):
         return pug.at[:, rows_c(half, zz), :]
@@ -105,13 +115,13 @@
     pr["own", 1] = rcopy(put.at[yl], pu_at(yl, z), right)
     ql["own", 1] = rcopy(put.at[yl], pu_at(yl, z), left)
     y_pu = rcopy(put.at[yo], pu_at(yl, z), mate)
-    pr["cu", 1] = rcopy(cu, cu_at(z), right)
-    ql["cu", 1] = rcopy(cu, cu_at(z), left)
-    here = []
-    for i, (src, dst) in enumerate([(put.at[yl], pu_at(yl, z)), (cu, cu_at(z)), (cd, cdb.at[my48, :])]):
-        copy = pltpu.make_async_copy(src, dst, lsem.at[i])
-        copy.start()
-        here.append(copy)
+    loads[1].wait()
+    pr["cu", 1] = rcopy(cu_at(z), cu_at(z), right)
+    ql["cu", 1] = rcopy(cu_at(z), cu_at(z), left)
+    keep = pltpu.make_async_copy(put.at[yl], pu_at(yl, z), lsem.at[8])
+    keep.start()
+    for load in loads[2:]:
+        load.wait()
     etb[:, yl] = jnp.transpose(et[...], (1, 0, 2))
     y_et = rcopy(etb.at[:, yl], etb.at[:, yl], mate)
     plb[my192, :] = jnp.transpose(low[...], (1, 0, 2)).reshape(ROWS, CHI)
@@ -122,7 +132,7 @@
     ql["oth", 1] = rcopy(pu_at(yo, z), pu_at(yo, z), left)
     elb[my192, :] = jnp.transpose(el[...], (1, 0, 2)).reshape(ROWS, CHI)
     y_el = rcopy(elb.at[my192, :], elb.at[my192, :], mate)
-    y_cd = rcopy(cd, cdb.at[my48, :], mate)
+    y_cd = rcopy(cdb.at[my48, :], cdb.at[my48, :], mate)
     ebb[my192, :] = jnp.transpose(eb[...], (1, 0, 2)).reshape(ROWS, CHI)
     y_eb = rcopy(ebb.at[my192, :], ebb.at[my192, :], mate)
 
@@ -166,9 +176,9 @@
     forward("own", 2)
     forward("oth", 2)
     lane = lax.broadcasted_iota(jnp.int32, (1, HALF), 1)
-    upper = jnp.where(lane >= ROWS, 1, 0)
-    rest = lane - upper * ROWS
-    target = 3 * 2 * BLK + upper * BLK + rest + lax.div(rest, BLK) * (HALF - BLK)
+    second = jnp.where(lane >= ROWS, 1, 0)
+    rest = lane - second * ROWS
+    target = 3 * 2 * BLK + second * BLK + rest + lax.div(rest, BLK) * (HALF - BLK)
     pick[...] = jnp.where(
         lax.broadcasted_iota(jnp.int32, pick.shape, 0) == target, 1.0, 0.0
     ).astype(BF)
@@ -176,8 +186,7 @@
     forward("cu", 3)
     forward("own", 3)
     forward("oth", 3)
-    for copy in here:
-        copy.wait()
+    keep.wait()
     y_et.wait_recv()
     forward("cu", 4)
     e2[...] = mul(cug[...], etb[...].reshape(HALF, CHI), 1, 1).astype(BF).reshape(ZN, BLK, HALF)
@@ -258,19 +267,20 @@
                 sbuf.at[side, t - 1, :, pl.ds(j0, n)], rbuf.at[side, t - 1, :, pl.ds(j0, n)], to
             )
 
-    outs = []
-
-    def rs_last(j0, n):
+    def rs_sum(j0, n, h):
+        value = own(j0, n, h, z)
+        for side in range(2):
+            value = value + rbuf[side, 3, h, j0:j0 + n].astype(F32)
+        return value.astype(BF)
+
+    def rs_end(j0):
         for side in range(2):
             flows[j0, side, 4].wait_recv()
-        for h in range(YN):
-            value = own(j0, n, h, z)
-            for side in range(2):
-                value = value + rbuf[side, 3, h, j0:j0 + n].astype(F32)
-            fin[h, j0:j0 + n] = value.astype(BF)
-        outs.append(rcopy(fin.at[yl, pl.ds(j0, n)], out.at[yl, pl.ds(j0, n)], at_bond(yl, z, dx=1)))
-        outs.append(rcopy(fin.at[yo, pl.ds(j0, n)], out.at[yl, pl.ds(j0, n)], at_bond(yo, z, dx=1)))
-
+
+    def deliver(src, dst):
+        return [rcopy(src.at[yl], dst, at_bond(yl, z, dx=1)), rcopy(src.at[yo], dst, at_bond(yo, z, dx=1))]
+
+    mylanes = pl.ds(pl.multiple_of(yl * HALF, 128), HALF)
     waves = [(0, 2), (2, 2), (4, 1), (5, 1)]
     lax.fori_loop(0, 2, edge_step, 0)
     rs_first(0, 2)
@@ -307,11 +317,21 @@
     for t in (3, 4):
         for j0, n in waves:
             rs_next(j0, n, t)
-    for j0, n in waves:
-        rs_last(j0, n)
-    for copy in outs:
-        copy.wait_recv()
-    for copy in started:
+    before = list(started)
+    rs_end(0)
+    rs_end(2)
+    for h in range(YN):
+        fin_edge[h] = jnp.transpose(rs_sum(0, D, h), (1, 0, 2))
+    outs = deliver(fin_edge, edge_out.at[:, :, mylanes])
+    rs_end(4)
+    for h in range(YN):
+        fin[h, 0] = rs_sum(D, 1, h)[0]
+    outs += deliver(fin.at[:, 0], lower_out.at[:, mylanes])
+    rs_end(5)
+    for h in range(YN):
+        fin[h, 1] = rs_sum(D + 1, 1, h)[0]
+    outs += deliver(fin.at[:, 1], upper_out.at[yl])
+    for copy in before:
         copy.wait_send()
     for dz in range(1, ZN):
         exchange(dz).wait_send()
@@ -320,30 +340,51 @@
     def _():
         exchange(0).wait_send()
 
-
-def arrange(parts, edge, lower, upper):
-    halves = [parts[0, :D], parts[1, :D]]
-    edge[...] = jnp.transpose(jnp.concatenate(halves, axis=2), (1, 0, 2))
-    lower[:, :HALF] = parts[0, D]
-    lower[:, HALF:] = parts[1, D]
-    first, second = parts[0, D + 1], parts[1, D + 1]
+    for copy in outs:
+        copy.wait_recv()
+    for copy in outs:
+        copy.wait_send()
+
+
+def settle(edge_in, lower_in, upper_in, edge_out, lower_out, upper_out, edge, lower, parts, upper, sems):
+    def move(i, src, dst):
+        copy = pltpu.make_async_copy(src, dst, sems.at[i])
+        copy.start()
+        return copy
+
+    arrived = [move(0, edge_in, edge), move(1, upper_in, parts), move(2, lower_in, lower)]
+    arrived[0].wait()
+    sent = [move(3, edge, edge_out)]
+    arrived[1].wait()
+    first, second = parts[0], parts[1]
     upper[...] = jnp.concatenate(
         [first[:, :ROWS], second[:, :ROWS], first[:, ROWS:], second[:, ROWS:]], axis=1
     )
+    sent.append(move(4, upper, upper_out))
+    arrived[2].wait()
+    sent.append(move(5, lower, lower_out))
+    for copy in sent:
+        copy.wait()
 
 
 def shards(
     corner_up, edge_top, edge_left, corner_down, edge_bottom, site_weights, proj_upper, proj_lower
 ):
-    vmem = pl.BlockSpec(memory_space=pltpu.VMEM)
     rows2 = YN * ROWS
     size = D * ROWS
-    parts = pl.pallas_call(
+    hbm = pl.BlockSpec(memory_space=pl.ANY)
+    edge, lower, upper = pl.pallas_call(
         kernel,
-        out_shape=jax.ShapeDtypeStruct((YN, SLABS, BLK, HALF), BF),
-        in_specs=[vmem] * 8,
-        out_specs=vmem,
+        out_shape=(
+            jax.ShapeDtypeStruct((BLK, D, CHI), BF),
+            jax.ShapeDtypeStruct((BLK, CHI), BF),
+            jax.ShapeDtypeStruct((YN, BLK, HALF), BF),
+        ),
+        in_specs=[hbm] * 8,
+        out_specs=(hbm,) * 3,
         scratch_shapes=[
+            *[pltpu.VMEM((BLK, D, CHI), BF)] * 5,
+            pltpu.VMEM((D, D, D, D), BF),
             pltpu.VMEM((YN, D, BLK, HALF), BF),
             pltpu.VMEM((D, CHI, HALF), BF),
             pltpu.VMEM((HALF, CHI), BF),
@@ -364,12 +405,13 @@
             pltpu.VMEM((SLABS, CHI, HALF), F32),
             pltpu.VMEM((2, 4, YN, SLABS, BLK, HALF), BF),
             pltpu.VMEM((2, 4, YN, SLABS, BLK, HALF), BF),
-            pltpu.VMEM((YN, SLABS, BLK, HALF), BF),
+            pltpu.VMEM((YN, 2, BLK, HALF), BF),
+            pltpu.VMEM((YN, BLK, D, HALF), BF),
             pltpu.SemaphoreType.DMA((COPIES,)),
             pltpu.SemaphoreType.DMA((COPIES,)),
             pltpu.SemaphoreType.DMA((ZN,)),
             pltpu.SemaphoreType.DMA((ZN,)),
-            pltpu.SemaphoreType.DMA((8,)),
+            pltpu.SemaphoreType.DMA((9,)),
         ],
         compiler_params=pltpu.CompilerParams(
             collective_id=0, has_side_effects=True, vmem_limit_bytes=56 * 1024 * 1024
@@ -379,15 +421,22 @@
         corner_up[0, 0], corner_down[0, 0], site_weights[0, 0],
     )
     edge, lower, upper = pl.pallas_call(
-        arrange,
+        settle,
         out_shape=(
             jax.ShapeDtypeStruct((BLK, D, CHI), BF),
             jax.ShapeDtypeStruct((BLK, CHI), BF),
             jax.ShapeDtypeStruct((BLK, CHI), BF),
         ),
-        in_specs=[vmem],
-        out_specs=(vmem, vmem, vmem),
-    )(parts)
+        in_specs=[hbm] * 3,
+        out_specs=(hbm,) * 3,
+        scratch_shapes=[
+            pltpu.VMEM((BLK, D, CHI), BF),
+            pltpu.VMEM((BLK, CHI), BF),
+            pltpu.VMEM((YN, BLK, HALF), BF),
+            pltpu.VMEM((BLK, CHI), BF),
+            pltpu.SemaphoreType.DMA((6,)),
+        ],
+    )(edge, lower, upper)
     return upper[None, None], edge[None, None], lower[None, None]
 
 

time: 91 us -> 89.4 us (0.982)
  Pallas kernels: 90.2 us -> 88.6 us
    pallas_call x2, Pallas kernels: 90.2 us -> 88.6 us  [the longest x1 86.8 us: shards(): pl.pallas_call(kernel, out_shape=(jax.ShapeDtypeStruct((BLK, D, CHI), BF)...]
where the time goes in v3:
time: 89.4 us; the launch traced here: 89.2 us
  Pallas kernels  88.6 us (99%)
    pallas_call x1, Pallas kernels, shards(): pl.pallas_call(kernel, out_shape=(jax.ShapeDtypeStruct((BLK, D, CHI), BF)...  86.8 us

profile of v3, /device:TPU:1, one launch (start us, length us, event | category | flops | bytes accessed | tf_op | source)
XLA Modules:
  0.0 89.2 jit_solution(5293385197851851632)
XLA Ops:
  0.6 86.8 %shard_map.103 = (bf16[48,4,768]{2,1,0:T(4,128)(2,1)}, bf16[48,768]{1,0:T(8,128)(2,1)}, bf16[2,48,384]{2,1,0:T(8,128)(2,1)}) custom-call(bf16[48,4,768]{2,1,0:T(4,128)(2,1)} %bitcast.11, bf16[48,4,768]{2,1,0:T(4,128)(2,1)} %bitcast.12, bf16[48,4,768]{2,1,0:T(4,128)(2,1)} %bitcast.13, bf16[48,4,768]{2,1,0:T(4,128)(2,1)} %bitcast.14, ...), custom_call_target="tpu_custom_call" | custom-call | tf_op jit(solution)/shard_map/pallas_call | solution.py:376
  87.5 1.8 %shard_map.104 = (bf16[48,4,768]{2,1,0:T(4,128)(2,1)}, bf16[48,768]{1,0:T(8,128)(2,1)}, bf16[48,768]{1,0:T(8,128)(2,1)}) custom-call(bf16[48,4,768]{2,1,0:T(4,128)(2,1)} %get-tuple-element.9.edge_in, bf16[48,768]{1,0:T(8,128)(2,1)} %get-tuple-element.10.lower_in, bf16[2,48,384]{2,1,0:T(8,128)(2,1)} %get-tuple-element.11.upper_in), custom_call_target="tpu_custom_call" | custom-call | tf_op jit(solution)/shard_map/pallas_call | solution.py:423

commit v4 on v3

--- a/solution.py
+++ b/solution.py
@@ -15,8 +15,13 @@
 BLK = CHI // (ZN * YN)
 HALF = CHI // YN
 ROWS = D * BLK
-SLABS = 6
-COPIES = 96
+LANE = 128
+CUTS = HALF // LANE
+TILE = 16
+LOWER = CUTS * D
+UPPER = LOWER + CUTS
+UNITS = UPPER + CUTS
+COPIES = 128
 
 
 def mul(a, b, ca=1, cb=0):
@@ -26,7 +31,7 @@
 def kernel(
     pu_in, low_in, el_in, et_in, eb_in, cu_in, cd_in, w_in,
     edge_out, lower_out, upper_out,
-    pu, low, el, et, eb, w, put, pug, cug, etb, elb, plb, lpb, ebb, cdb, mix, xb, fb, lb, pick, e2, er, ebuf, outp, sbuf, rbuf, fin, fin_edge,
+    pu, low, el, et, eb, w, put, pug, cug, etb, elb, plb, lpb, ebb, cdb, mix, xb, fb, lpt, lb, pick, e2, er, ebuf, outp, sbuf, rbuf, fin, fin_edge,
     ssem, rsem, asem, bsem, lsem,
 ):
     bond = lax.axis_index("bond")
@@ -152,10 +157,10 @@
 
     forward("own", 1)
     forward("cu", 1)
-    size = D * D * BLK
+    size = D * D * TILE
     rowi = lax.broadcasted_iota(jnp.int32, (size, D ** 3), 0)
     coli = lax.broadcasted_iota(jnp.int32, (size, D ** 3), 1)
-    legs = lax.rem(lax.div(rowi, BLK), D) * D + lax.div(rowi, ROWS)
+    legs = lax.rem(lax.div(rowi, TILE), D) * D + lax.div(rowi, D * TILE)
     weights = w[...].reshape(D ** 3, D)
     spread = jnp.zeros((size, D * D), F32)
     for l in range(D):
@@ -165,16 +170,19 @@
         spread = spread + mul(mul(one, weights).astype(BF), jnp.where(col == d_at, 1.0, 0.0).astype(BF))
     leg = lax.broadcasted_iota(jnp.int32, (D * D, size), 0)
     pos = lax.broadcasted_iota(jnp.int32, (D * D, size), 1)
-    expand = jnp.where(leg == lax.div(pos, BLK), 1.0, 0.0).astype(BF)
+    expand = jnp.where(leg == lax.div(pos, TILE), 1.0, 0.0).astype(BF)
     full = mul(spread.astype(BF), expand)
-    inrow = lax.rem(lax.broadcasted_iota(jnp.int32, (size, 1), 0), BLK)
-    incol = lax.rem(lax.broadcasted_iota(jnp.int32, (1, size), 1), BLK)
+    inrow = lax.rem(lax.broadcasted_iota(jnp.int32, (size, 1), 0), TILE)
+    incol = lax.rem(lax.broadcasted_iota(jnp.int32, (1, size), 1), TILE)
     mix[...] = jnp.where(inrow == incol, full, 0.0).astype(BF)
 
     forward("oth", 1)
     forward("cu", 2)
     forward("own", 2)
     forward("oth", 2)
+    x_same.wait_recv()
+    x_other.wait_recv()
+    lpt[...] = lpb[...].T
     lane = lax.broadcasted_iota(jnp.int32, (1, HALF), 1)
     second = jnp.where(lane >= ROWS, 1, 0)
     rest = lane - second * ROWS
@@ -218,28 +226,28 @@
     y_el.wait_recv()
     y_cd.wait_recv()
 
-    def x_step(d, carry):
+    for d in range(D):
         x = mul(elb[...], pug[d]).astype(BF)
-        base = pl.multiple_of(d * ROWS, 16)
-        xb[0, pl.ds(base, ROWS), :] = x[:ROWS]
-        xb[1, pl.ds(base, ROWS), :] = x[ROWS:]
-        return carry
-
-    lax.fori_loop(0, D, x_step, 0)
-
-    def mix_step(h, carry):
-        f = mul(mix[...], xb[h]).astype(BF)
+        for h in range(YN):
+            for l in range(D):
+                for c in range(BLK // TILE):
+                    row = h * ROWS + l * BLK + c * TILE
+                    to = (d * D + l) * TILE
+                    xb[h, c, to:to + TILE, :] = x[row:row + TILE]
+    for h in range(YN):
+        for c in range(BLK // TILE):
+            f = mul(mix[...], xb[h, c]).astype(BF)
+            for i in range(CUTS):
+                for r in range(D):
+                    for u in range(D):
+                        row = h * ROWS + u * BLK + c * TILE
+                        part = f[(r * D + u) * TILE:(r * D + u + 1) * TILE, i * LANE:(i + 1) * LANE]
+                        fb[i, row:row + TILE, r * LANE:(r + 1) * LANE] = part
+
+    def edge_step(i):
+        part = mul(lpt[...], fb[i])
         for r in range(D):
-            fb[r, pl.ds(pl.multiple_of(h * ROWS, 16), ROWS), :] = f[r * ROWS:(r + 1) * ROWS]
-        return carry
-
-    lax.fori_loop(0, YN, mix_step, 0)
-    x_same.wait_recv()
-    x_other.wait_recv()
-
-    def edge_step(r, carry):
-        outp[r] = mul(lpb[...], fb[r], 0, 0)
-        return carry
+            outp[i * D + r] = part[:, r * LANE:(r + 1) * LANE]
 
     def own(j0, n, h, zz):
         return outp[j0:j0 + n, pl.ds(pl.multiple_of(h * HALF + zz * BLK, 16), BLK), :]
@@ -280,12 +288,10 @@
     def deliver(src, dst):
         return [rcopy(src.at[yl], dst, at_bond(yl, z, dx=1)), rcopy(src.at[yo], dst, at_bond(yo, z, dx=1))]
 
-    mylanes = pl.ds(pl.multiple_of(yl * HALF, 128), HALF)
-    waves = [(0, 2), (2, 2), (4, 1), (5, 1)]
-    lax.fori_loop(0, 2, edge_step, 0)
-    rs_first(0, 2)
-    lax.fori_loop(2, 4, edge_step, 0)
-    rs_first(2, 2)
+    waves = [(i * D, D) for i in range(CUTS)] + [(LOWER, CUTS), (UPPER, CUTS)]
+    for i in range(CUTS):
+        edge_step(i)
+        rs_first(i * D, D)
 
     def low_step(d, carry):
         part = mul(cdb[...], pug[d]).astype(BF)
@@ -295,9 +301,11 @@
 
     lax.fori_loop(0, D, low_step, 0)
     y_eb.wait_recv()
-    outp[4] = mul(ebb[...], lb[...], 0, 0)
-    rs_first(4, 1)
-    rs_next(0, 2, 2)
+    part = mul(ebb[...], lb[...], 0, 0)
+    for i in range(CUTS):
+        outp[LOWER + i] = part[:, i * LANE:(i + 1) * LANE]
+    rs_first(LOWER, CUTS)
+    rs_next(0, D, 2)
     for half in range(YN):
         for q in range(ZN // 2):
             pltpu.make_async_copy(e2.at[0], er_at(half, q), bsem.at[half * (ZN // 2) + q]).wait()
@@ -310,27 +318,32 @@
         return carry
 
     lax.fori_loop(0, D, pick_step, 0)
-    outp[5] = mul(lpb[...], ebuf[...], 0, 0)
-    rs_first(5, 1)
+    part = mul(lpt[...], ebuf[...])
+    for i in range(CUTS):
+        outp[UPPER + i] = part[:, i * LANE:(i + 1) * LANE]
+    rs_first(UPPER, CUTS)
     for j0, n in waves[1:]:
         rs_next(j0, n, 2)
     for t in (3, 4):
         for j0, n in waves:
             rs_next(j0, n, t)
     before = list(started)
-    rs_end(0)
-    rs_end(2)
-    for h in range(YN):
-        fin_edge[h] = jnp.transpose(rs_sum(0, D, h), (1, 0, 2))
-    outs = deliver(fin_edge, edge_out.at[:, :, mylanes])
-    rs_end(4)
-    for h in range(YN):
-        fin[h, 0] = rs_sum(D, 1, h)[0]
-    outs += deliver(fin.at[:, 0], lower_out.at[:, mylanes])
-    rs_end(5)
-    for h in range(YN):
-        fin[h, 1] = rs_sum(D + 1, 1, h)[0]
-    outs += deliver(fin.at[:, 1], upper_out.at[yl])
+    outs = []
+    for i in range(CUTS):
+        rs_end(i * D)
+        for h in range(YN):
+            fin_edge[i, h] = jnp.transpose(rs_sum(i * D, D, h), (1, 0, 2))
+        lanes = pl.ds(pl.multiple_of(yl * HALF + i * LANE, LANE), LANE)
+        outs += deliver(fin_edge.at[i], edge_out.at[:, :, lanes])
+    for j, (j0, dst) in enumerate((
+        (LOWER, lower_out.at[:, pl.ds(pl.multiple_of(yl * HALF, LANE), HALF)]), (UPPER, upper_out.at[yl])
+    )):
+        rs_end(j0)
+        for h in range(YN):
+            total = rs_sum(j0, CUTS, h)
+            for i in range(CUTS):
+                fin[j, h, :, i * LANE:(i + 1) * LANE] = total[i]
+        outs += deliver(fin.at[j], dst)
     for copy in before:
         copy.wait_send()
     for dz in range(1, ZN):
@@ -371,7 +384,7 @@
     corner_up, edge_top, edge_left, corner_down, edge_bottom, site_weights, proj_upper, proj_lower
 ):
     rows2 = YN * ROWS
-    size = D * ROWS
+    size = D * D * TILE
     hbm = pl.BlockSpec(memory_space=pl.ANY)
     edge, lower, upper = pl.pallas_call(
         kernel,
@@ -395,18 +408,19 @@
             pltpu.VMEM((rows2, CHI), BF),
             pltpu.VMEM((YN * BLK, CHI), BF),
             pltpu.VMEM((size, size), BF),
-            pltpu.VMEM((YN, size, HALF), BF),
-            pltpu.VMEM((D, rows2, HALF), BF),
+            pltpu.VMEM((YN, BLK // TILE, size, HALF), BF),
+            pltpu.VMEM((CUTS, rows2, D * LANE), BF),
+            pltpu.VMEM((CHI, rows2), BF),
             pltpu.VMEM((rows2, HALF), BF),
             pltpu.VMEM((4 * HALF + 6 * BLK, HALF), BF),
             pltpu.VMEM((ZN, BLK, HALF), BF),
             pltpu.VMEM((YN, BLK, 4 * HALF), BF),
             pltpu.VMEM((rows2, HALF), BF),
-            pltpu.VMEM((SLABS, CHI, HALF), F32),
-            pltpu.VMEM((2, 4, YN, SLABS, BLK, HALF), BF),
-            pltpu.VMEM((2, 4, YN, SLABS, BLK, HALF), BF),
-            pltpu.VMEM((YN, 2, BLK, HALF), BF),
-            pltpu.VMEM((YN, BLK, D, HALF), BF),
+            pltpu.VMEM((UNITS, CHI, LANE), F32),
+            pltpu.VMEM((2, 4, YN, UNITS, BLK, LANE), BF),
+            pltpu.VMEM((2, 4, YN, UNITS, BLK, LANE), BF),
+            pltpu.VMEM((2, YN, BLK, HALF), BF),
+            pltpu.VMEM((CUTS, YN, BLK, D, LANE), BF),
             pltpu.SemaphoreType.DMA((COPIES,)),
             pltpu.SemaphoreType.DMA((COPIES,)),
             pltpu.SemaphoreType.DMA((ZN,)),

time: 89.4 us -> 87.1 us (0.974)
  Pallas kernels: 88.6 us -> 86.4 us
    pallas_call x1, Pallas kernels: 86.8 us -> 84.6 us  [shards(): pl.pallas_call(kernel, out_shape=(jax.ShapeDtypeStruct((BLK, D, CHI), BF)...]
where the time goes in v4:
time: 87.1 us; the launch traced here: 87 us
  Pallas kernels  86.4 us (99%)
    pallas_call x1, Pallas kernels, shards(): pl.pallas_call(kernel, out_shape=(jax.ShapeDtypeStruct((BLK, D, CHI), BF)...  84.6 us
    pallas_call x1, Pallas kernels, shards(): pl.pallas_call(settle, out_shape=(jax.ShapeDtypeStruct((BLK, D, CHI), BF)...  1.77 us

profile of v4, /device:TPU:1, one launch (start us, length us, event | category | flops | bytes accessed | tf_op | source)
XLA Modules:
  0.0 87.0 jit_solution(18443023595287451157)
XLA Ops:
  0.6 84.6 %shard_map.103 = (bf16[48,4,768]{2,1,0:T(4,128)(2,1)}, bf16[48,768]{1,0:T(8,128)(2,1)}, bf16[2,48,384]{2,1,0:T(8,128)(2,1)}) custom-call(bf16[48,4,768]{2,1,0:T(4,128)(2,1)} %bitcast.11, bf16[48,4,768]{2,1,0:T(4,128)(2,1)} %bitcast.12, bf16[48,4,768]{2,1,0:T(4,128)(2,1)} %bitcast.13, bf16[48,4,768]{2,1,0:T(4,128)(2,1)} %bitcast.14, ...), custom_call_target="tpu_custom_call" | custom-call | tf_op jit(solution)/shard_map/pallas_call | solution.py:389
  85.3 1.8 %shard_map.104 = (bf16[48,4,768]{2,1,0:T(4,128)(2,1)}, bf16[48,768]{1,0:T(8,128)(2,1)}, bf16[48,768]{1,0:T(8,128)(2,1)}) custom-call(bf16[48,4,768]{2,1,0:T(4,128)(2,1)} %get-tuple-element.9.edge_in, bf16[48,768]{1,0:T(8,128)(2,1)} %get-tuple-element.10.lower_in, bf16[2,48,384]{2,1,0:T(8,128)(2,1)} %get-tuple-element.11.upper_in), custom_call_target="tpu_custom_call" | custom-call | tf_op jit(solution)/shard_map/pallas_call | solution.py:437

commit v5 on v4

--- a/solution.py
+++ b/solution.py
@@ -21,7 +21,8 @@
 LOWER = CUTS * D
 UPPER = LOWER + CUTS
 UNITS = UPPER + CUTS
-COPIES = 128
+COPIES = 79
+SENDS = 24
 
 
 def mul(a, b, ca=1, cb=0):
@@ -87,13 +88,13 @@
     pl.semaphore_wait(barrier, len(sources) + ZN - jnp.where(zh == yl, 1, 0))
 
     started = []
-    count = [0]
 
     def rcopy(src, dst, to):
-        index = count[0]
-        count[0] += 1
+        index = len(started)
+        if index >= SENDS:
+            started[index - SENDS].wait_send()
         copy = pltpu.make_async_remote_copy(
-            src_ref=src, dst_ref=dst, send_sem=ssem.at[index], recv_sem=rsem.at[index],
+            src_ref=src, dst_ref=dst, send_sem=ssem.at[index % SENDS], recv_sem=rsem.at[index],
             device_id=to, device_id_type=MESH,
         )
         copy.start()
@@ -202,11 +203,9 @@
     def er_at(half, q):
         return er.at[half, :, pl.ds(pl.multiple_of(q * HALF, 128), HALF)]
 
-    slot = yl * (ZN // 2) + zq
-
     def exchange(dz):
         return pltpu.make_async_remote_copy(
-            src_ref=e2.at[zmod(dz)], dst_ref=er_at(yl, zq), send_sem=asem.at[dz], recv_sem=bsem.at[slot],
+            src_ref=e2.at[zmod(dz)], dst_ref=er_at(yl, zq), send_sem=asem.at[min(dz, 1)], recv_sem=bsem,
             device_id=at_bond(zh, zmod(dz)), device_id_type=MESH,
         )
 
@@ -215,7 +214,7 @@
 
     @pl.when(zh == yl)
     def _():
-        pltpu.make_async_copy(e2.at[z], er_at(yl, zq), bsem.at[slot]).start()
+        pltpu.make_async_copy(e2.at[z], er_at(yl, zq), bsem).start()
 
     @pl.when(zh != yl)
     def _():
@@ -306,9 +305,7 @@
         outp[LOWER + i] = part[:, i * LANE:(i + 1) * LANE]
     rs_first(LOWER, CUTS)
     rs_next(0, D, 2)
-    for half in range(YN):
-        for q in range(ZN // 2):
-            pltpu.make_async_copy(e2.at[0], er_at(half, q), bsem.at[half * (ZN // 2) + q]).wait()
+    pltpu.make_async_copy(er, er, bsem).wait()
 
     def pick_step(k, carry):
         shift = pl.multiple_of((3 - k) * 2 * BLK, 16)
@@ -327,7 +324,6 @@
     for t in (3, 4):
         for j0, n in waves:
             rs_next(j0, n, t)
-    before = list(started)
     outs = []
     for i in range(CUTS):
         rs_end(i * D)
@@ -344,10 +340,8 @@
             for i in range(CUTS):
                 fin[j, h, :, i * LANE:(i + 1) * LANE] = total[i]
         outs += deliver(fin.at[j], dst)
-    for copy in before:
-        copy.wait_send()
-    for dz in range(1, ZN):
-        exchange(dz).wait_send()
+    rest = e2.at[pl.ds(1, ZN - 1)]
+    pltpu.make_async_copy(rest, rest, asem.at[1]).wait()
 
     @pl.when(zh != yl)
     def _():
@@ -355,7 +349,7 @@
 
     for copy in outs:
         copy.wait_recv()
-    for copy in outs:
+    for copy in started[-SENDS:]:
         copy.wait_send()
 
 
@@ -421,10 +415,10 @@
             pltpu.VMEM((2, 4, YN, UNITS, BLK, LANE), BF),
             pltpu.VMEM((2, YN, BLK, HALF), BF),
             pltpu.VMEM((CUTS, YN, BLK, D, LANE), BF),
+            pltpu.SemaphoreType.DMA((SENDS,)),
             pltpu.SemaphoreType.DMA((COPIES,)),
-            pltpu.SemaphoreType.DMA((COPIES,)),
-            pltpu.SemaphoreType.DMA((ZN,)),
-            pltpu.SemaphoreType.DMA((ZN,)),
+            pltpu.SemaphoreType.DMA((2,)),
+            pltpu.SemaphoreType.DMA,
             pltpu.SemaphoreType.DMA((9,)),
         ],
         compiler_params=pltpu.CompilerParams(

time: 87.1 us -> 85.7 us (0.984)
  Pallas kernels: 86.4 us -> 85 us
    pallas_call x1, Pallas kernels: 84.6 us -> 83.2 us  [shards(): pl.pallas_call(kernel, out_shape=(jax.ShapeDtypeStruct((BLK, D, CHI), BF)...]
where the time goes in v5:
time: 85.7 us; the launch traced here: 85.6 us
  Pallas kernels  85 us (99%)
    pallas_call x1, Pallas kernels, shards(): pl.pallas_call(kernel, out_shape=(jax.ShapeDtypeStruct((BLK, D, CHI), BF)...  83.2 us
    pallas_call x1, Pallas kernels, shards(): pl.pallas_call(settle, out_shape=(jax.ShapeDtypeStruct((BLK, D, CHI), BF)...  1.77 us

profile of v5, /device:TPU:1, one launch (start us, length us, event | category | flops | bytes accessed | tf_op | source)
XLA Modules:
  0.0 85.6 jit_solution(9828123601652202923)
XLA Ops:
  0.6 83.2 %shard_map.103 = (bf16[48,4,768]{2,1,0:T(4,128)(2,1)}, bf16[48,768]{1,0:T(8,128)(2,1)}, bf16[2,48,384]{2,1,0:T(8,128)(2,1)}) custom-call(bf16[48,4,768]{2,1,0:T(4,128)(2,1)} %bitcast.11, bf16[48,4,768]{2,1,0:T(4,128)(2,1)} %bitcast.12, bf16[48,4,768]{2,1,0:T(4,128)(2,1)} %bitcast.13, bf16[48,4,768]{2,1,0:T(4,128)(2,1)} %bitcast.14, ...), custom_call_target="tpu_custom_call" | custom-call | tf_op jit(solution)/shard_map/pallas_call | solution.py:383
  83.8 1.8 %shard_map.104 = (bf16[48,4,768]{2,1,0:T(4,128)(2,1)}, bf16[48,768]{1,0:T(8,128)(2,1)}, bf16[48,768]{1,0:T(8,128)(2,1)}) custom-call(bf16[48,4,768]{2,1,0:T(4,128)(2,1)} %get-tuple-element.9.edge_in, bf16[48,768]{1,0:T(8,128)(2,1)} %get-tuple-element.10.lower_in, bf16[2,48,384]{2,1,0:T(8,128)(2,1)} %get-tuple-element.11.upper_in), custom_call_target="tpu_custom_call" | custom-call | tf_op jit(solution)/shard_map/pallas_call | solution.py:431

commit v6 on v5

--- a/solution.py
+++ b/solution.py
@@ -21,8 +21,8 @@
 LOWER = CUTS * D
 UPPER = LOWER + CUTS
 UNITS = UPPER + CUTS
-COPIES = 79
-SENDS = 24
+RECVS = 43
+SENDS = 28
 
 
 def mul(a, b, ca=1, cb=0):
@@ -89,18 +89,27 @@
 
     started = []
 
-    def rcopy(src, dst, to):
+    used = [0]
+
+    def fresh():
+        used[0] += 1
+        return rsem.at[used[0] - 1]
+
+    def rcopy(src, dst, to, sem):
         index = len(started)
         if index >= SENDS:
             started[index - SENDS].wait_send()
         copy = pltpu.make_async_remote_copy(
-            src_ref=src, dst_ref=dst, send_sem=ssem.at[index % SENDS], recv_sem=rsem.at[index],
+            src_ref=src, dst_ref=dst, send_sem=ssem.at[index % SENDS], recv_sem=sem,
             device_id=to, device_id_type=MESH,
         )
         copy.start()
         started.append(copy)
         return copy
 
+    def take(like, sem):
+        pltpu.make_async_copy(like, like, sem).wait()
+
     def rows_c(half, zz):
         return pl.ds(pl.multiple_of(half * HALF + zz * BLK, 16), BLK)
 
@@ -117,44 +126,55 @@
             return cug.at[rows_z(zz), :]
         return cug.at[rows_z(zz), pl.ds(part * HALF, HALF)]
 
-    pr, ql = {}, {}
-    pr["own", 1] = rcopy(put.at[yl], pu_at(yl, z), right)
-    ql["own", 1] = rcopy(put.at[yl], pu_at(yl, z), left)
-    y_pu = rcopy(put.at[yo], pu_at(yl, z), mate)
+    ring = {}
+    for name in ("own", "oth", "cu"):
+        for m in range(1, 5):
+            ring[name, m] = fresh()
+
+    def both(name, m, at_right, at_left):
+        for at, to in ((at_right, right), (at_left, left)):
+            if at is not None:
+                rcopy(at[0], at[1], to, ring[name, m])
+
+    both("own", 1, (put.at[yl], pu_at(yl, z)), (put.at[yl], pu_at(yl, z)))
+    y_pu = rcopy(put.at[yo], pu_at(yl, z), mate, fresh())
     loads[1].wait()
-    pr["cu", 1] = rcopy(cu_at(z), cu_at(z), right)
-    ql["cu", 1] = rcopy(cu_at(z), cu_at(z), left)
+    both("cu", 1, (cu_at(z), cu_at(z)), (cu_at(z), cu_at(z)))
     keep = pltpu.make_async_copy(put.at[yl], pu_at(yl, z), lsem.at[8])
     keep.start()
     for load in loads[2:]:
         load.wait()
     etb[:, yl] = jnp.transpose(et[...], (1, 0, 2))
-    y_et = rcopy(etb.at[:, yl], etb.at[:, yl], mate)
+    y_et = rcopy(etb.at[:, yl], etb.at[:, yl], mate, fresh())
     plb[my192, :] = jnp.transpose(low[...], (1, 0, 2)).reshape(ROWS, CHI)
-    x_same = rcopy(plb.at[my192, :], lpb.at[my192, :], at_bond(yl, z, dy=1))
-    x_other = rcopy(plb.at[my192, :], lpb.at[my192, :], at_bond(yo, z, dy=1))
+    x_sem = fresh()
+    for half in (yl, yo):
+        rcopy(plb.at[my192, :], lpb.at[my192, :], at_bond(half, z, dy=1), x_sem)
     y_pu.wait_recv()
-    pr["oth", 1] = rcopy(pu_at(yo, z), pu_at(yo, z), right)
-    ql["oth", 1] = rcopy(pu_at(yo, z), pu_at(yo, z), left)
+    both("oth", 1, (pu_at(yo, z), pu_at(yo, z)), (pu_at(yo, z), pu_at(yo, z)))
     elb[my192, :] = jnp.transpose(el[...], (1, 0, 2)).reshape(ROWS, CHI)
-    y_el = rcopy(elb.at[my192, :], elb.at[my192, :], mate)
-    y_cd = rcopy(cdb.at[my48, :], cdb.at[my48, :], mate)
+    y_el = rcopy(elb.at[my192, :], elb.at[my192, :], mate, fresh())
+    y_cd = rcopy(cdb.at[my48, :], cdb.at[my48, :], mate, fresh())
     ebb[my192, :] = jnp.transpose(eb[...], (1, 0, 2)).reshape(ROWS, CHI)
-    y_eb = rcopy(ebb.at[my192, :], ebb.at[my192, :], mate)
+    y_eb = rcopy(ebb.at[my192, :], ebb.at[my192, :], mate, fresh())
 
     def forward(name, m):
-        for flow, sign, to, last in ((pr, -1, right, "own"), (ql, 1, left, "oth")):
-            if (name, m) not in flow:
-                continue
-            flow[name, m].wait_recv()
-            zz = zmod(sign * m)
-            if name == "cu":
-                if m < 4:
-                    at = cu_at(zz) if m < 3 else cu_at(zz, 0 if last == "own" else 1)
-                    flow[name, m + 1] = rcopy(at, at, to)
-            elif m < 3 or (m == 3 and name == last):
-                at = pu_at(yl if name == "own" else yo, zz)
-                flow[name, m + 1] = rcopy(at, at, to)
+        if name == "cu":
+            like = cug.at[pl.ds(0, BLK if m == 4 else 2 * BLK), :]
+        else:
+            like = put.at[0] if m == 4 else put
+        take(like, ring[name, m])
+        if m == 4:
+            return
+        if name == "cu":
+            cuts = (None, None) if m < 3 else (0, 1)
+            ats = [cu_at(zmod(-m), cuts[0]), cu_at(zmod(m), cuts[1])]
+        else:
+            half = yl if name == "own" else yo
+            ats = [pu_at(half, zmod(-m)), pu_at(half, zmod(m))]
+            if m == 3:
+                ats[1 if name == "own" else 0] = None
+        both(name, m + 1, *[None if at is None else (at, at) for at in ats])
 
     forward("own", 1)
     forward("cu", 1)
@@ -181,9 +201,6 @@
     forward("cu", 2)
     forward("own", 2)
     forward("oth", 2)
-    x_same.wait_recv()
-    x_other.wait_recv()
-    lpt[...] = lpb[...].T
     lane = lax.broadcasted_iota(jnp.int32, (1, HALF), 1)
     second = jnp.where(lane >= ROWS, 1, 0)
     rest = lane - second * ROWS
@@ -209,7 +226,7 @@
             device_id=at_bond(zh, zmod(dz)), device_id_type=MESH,
         )
 
-    for dz in (4, 3, 5, 2, 6, 1, 7):
+    for dz in (1, 7, 2, 6, 3, 5, 4):
         exchange(dz).start()
 
     @pl.when(zh == yl)
@@ -220,6 +237,8 @@
     def _():
         exchange(0).start()
 
+    take(lpb, x_sem)
+    lpt[...] = lpb[...].T
     forward("own", 4)
     forward("oth", 4)
     y_el.wait_recv()
@@ -251,27 +270,32 @@
     def own(j0, n, h, zz):
         return outp[j0:j0 + n, pl.ds(pl.multiple_of(h * HALF + zz * BLK, 16), BLK), :]
 
-    flows = {}
+    sums = {}
+
+    def rs_take(j0, n, t):
+        take(rbuf.at[:, t - 1, :, pl.ds(j0, n)] if t > 1 else rbuf.at[0, 0, :, pl.ds(j0, n)], sums[j0, t])
 
     def rs_first(j0, n):
         zz = zmod(4)
+        sums[j0, 1] = fresh()
         for side, h, to in ((0, 0, right), (1, 1, left)):
             sbuf[side, 0, h, j0:j0 + n] = own(j0, n, h, zz).astype(BF)
-            flows[j0, side, 1] = rcopy(
-                sbuf.at[side, 0, h, pl.ds(j0, n)], rbuf.at[side, 0, h, pl.ds(j0, n)], to
+            rcopy(
+                sbuf.at[side, 0, h, pl.ds(j0, n)], rbuf.at[side, 0, h, pl.ds(j0, n)], to, sums[j0, 1]
             )
 
     def rs_next(j0, n, t):
+        rs_take(j0, n, t - 1)
+        sums[j0, t] = fresh()
         for side, sign, to in ((0, 1, right), (1, -1, left)):
-            flows[j0, side, t - 1].wait_recv()
             zz = zmod(sign * (5 - t))
             for h in range(YN):
                 value = own(j0, n, h, zz)
                 if t > 2 or h == side:
                     value = value + rbuf[side, t - 2, h, j0:j0 + n].astype(F32)
                 sbuf[side, t - 1, h, j0:j0 + n] = value.astype(BF)
-            flows[j0, side, t] = rcopy(
-                sbuf.at[side, t - 1, :, pl.ds(j0, n)], rbuf.at[side, t - 1, :, pl.ds(j0, n)], to
+            rcopy(
+                sbuf.at[side, t - 1, :, pl.ds(j0, n)], rbuf.at[side, t - 1, :, pl.ds(j0, n)], to, sums[j0, t]
             )
 
     def rs_sum(j0, n, h):
@@ -280,12 +304,11 @@
             value = value + rbuf[side, 3, h, j0:j0 + n].astype(F32)
         return value.astype(BF)
 
-    def rs_end(j0):
-        for side in range(2):
-            flows[j0, side, 4].wait_recv()
-
     def deliver(src, dst):
-        return [rcopy(src.at[yl], dst, at_bond(yl, z, dx=1)), rcopy(src.at[yo], dst, at_bond(yo, z, dx=1))]
+        sem = fresh()
+        for half in (yl, yo):
+            rcopy(src.at[half], dst, at_bond(half, z, dx=1), sem)
+        return [(src, sem)]
 
     waves = [(i * D, D) for i in range(CUTS)] + [(LOWER, CUTS), (UPPER, CUTS)]
     for i in range(CUTS):
@@ -326,7 +349,7 @@
             rs_next(j0, n, t)
     outs = []
     for i in range(CUTS):
-        rs_end(i * D)
+        rs_take(i * D, D, 4)
         for h in range(YN):
             fin_edge[i, h] = jnp.transpose(rs_sum(i * D, D, h), (1, 0, 2))
         lanes = pl.ds(pl.multiple_of(yl * HALF + i * LANE, LANE), LANE)
@@ -334,7 +357,7 @@
     for j, (j0, dst) in enumerate((
         (LOWER, lower_out.at[:, pl.ds(pl.multiple_of(yl * HALF, LANE), HALF)]), (UPPER, upper_out.at[yl])
     )):
-        rs_end(j0)
+        rs_take(j0, CUTS, 4)
         for h in range(YN):
             total = rs_sum(j0, CUTS, h)
             for i in range(CUTS):
@@ -347,8 +370,8 @@
     def _():
         exchange(0).wait_send()
 
-    for copy in outs:
-        copy.wait_recv()
+    for like, sem in outs:
+        take(like, sem)
     for copy in started[-SENDS:]:
         copy.wait_send()
 
@@ -416,7 +439,7 @@
             pltpu.VMEM((2, YN, BLK, HALF), BF),
             pltpu.VMEM((CUTS, YN, BLK, D, LANE), BF),
             pltpu.SemaphoreType.DMA((SENDS,)),
-            pltpu.SemaphoreType.DMA((COPIES,)),
+            pltpu.SemaphoreType.DMA((RECVS,)),
             pltpu.SemaphoreType.DMA((2,)),
             pltpu.SemaphoreType.DMA,
             pltpu.SemaphoreType.DMA((9,)),

time: 85.7 us -> 85.3 us (level)
  no operation moved by 1% of the time
where the time goes in v6:
time: 85.3 us; the launch traced here: 85.2 us
  Pallas kernels  84.6 us (99%)
    pallas_call x1, Pallas kernels, shards(): pl.pallas_call(kernel, out_shape=(jax.ShapeDtypeStruct((BLK, D, CHI), BF)...  82.8 us
    pallas_call x1, Pallas kernels, shards(): pl.pallas_call(settle, out_shape=(jax.ShapeDtypeStruct((BLK, D, CHI), BF)...  1.77 us

profile of v6, /device:TPU:1, one launch (start us, length us, event | category | flops | bytes accessed | tf_op | source)
XLA Modules:
  0.0 85.2 jit_solution(852874052680824975)
XLA Ops:
  0.6 82.8 %shard_map.103 = (bf16[48,4,768]{2,1,0:T(4,128)(2,1)}, bf16[48,768]{1,0:T(8,128)(2,1)}, bf16[2,48,384]{2,1,0:T(8,128)(2,1)}) custom-call(bf16[48,4,768]{2,1,0:T(4,128)(2,1)} %bitcast.11, bf16[48,4,768]{2,1,0:T(4,128)(2,1)} %bitcast.12, bf16[48,4,768]{2,1,0:T(4,128)(2,1)} %bitcast.13, bf16[48,4,768]{2,1,0:T(4,128)(2,1)} %bitcast.14, ...), custom_call_target="tpu_custom_call" | custom-call | tf_op jit(solution)/shard_map/pallas_call | solution.py:406
  83.5 1.8 %shard_map.104 = (bf16[48,4,768]{2,1,0:T(4,128)(2,1)}, bf16[48,768]{1,0:T(8,128)(2,1)}, bf16[48,768]{1,0:T(8,128)(2,1)}) custom-call(bf16[48,4,768]{2,1,0:T(4,128)(2,1)} %get-tuple-element.9.edge_in, bf16[48,768]{1,0:T(8,128)(2,1)} %get-tuple-element.10.lower_in, bf16[2,48,384]{2,1,0:T(8,128)(2,1)} %get-tuple-element.11.upper_in), custom_call_target="tpu_custom_call" | custom-call | tf_op jit(solution)/shard_map/pallas_call | solution.py:454

commit v7 on v6

--- a/solution.py
+++ b/solution.py
@@ -21,7 +21,7 @@
 LOWER = CUTS * D
 UPPER = LOWER + CUTS
 UNITS = UPPER + CUTS
-RECVS = 43
+RECVS = 51
 SENDS = 28
 
 
@@ -136,10 +136,10 @@
             if at is not None:
                 rcopy(at[0], at[1], to, ring[name, m])
 
+    loads[1].wait()
+    both("cu", 1, (cu_at(z), cu_at(z)), (cu_at(z), cu_at(z)))
     both("own", 1, (put.at[yl], pu_at(yl, z)), (put.at[yl], pu_at(yl, z)))
     y_pu = rcopy(put.at[yo], pu_at(yl, z), mate, fresh())
-    loads[1].wait()
-    both("cu", 1, (cu_at(z), cu_at(z)), (cu_at(z), cu_at(z)))
     keep = pltpu.make_async_copy(put.at[yl], pu_at(yl, z), lsem.at[8])
     keep.start()
     for load in loads[2:]:
@@ -176,8 +176,8 @@
                 ats[1 if name == "own" else 0] = None
         both(name, m + 1, *[None if at is None else (at, at) for at in ats])
 
+    forward("cu", 1)
     forward("own", 1)
-    forward("cu", 1)
     size = D * D * TILE
     rowi = lax.broadcasted_iota(jnp.int32, (size, D ** 3), 0)
     coli = lax.broadcasted_iota(jnp.int32, (size, D ** 3), 1)
@@ -284,8 +284,9 @@
                 sbuf.at[side, 0, h, pl.ds(j0, n)], rbuf.at[side, 0, h, pl.ds(j0, n)], to, sums[j0, 1]
             )
 
-    def rs_next(j0, n, t):
-        rs_take(j0, n, t - 1)
+    def rs_next(j0, n, t, taken=False):
+        if not taken:
+            rs_take(j0, n, t - 1)
         sums[j0, t] = fresh()
         for side, sign, to in ((0, 1, right), (1, -1, left)):
             zz = zmod(sign * (5 - t))
@@ -344,9 +345,14 @@
     rs_first(UPPER, CUTS)
     for j0, n in waves[1:]:
         rs_next(j0, n, 2)
-    for t in (3, 4):
-        for j0, n in waves:
-            rs_next(j0, n, t)
+    for j0, n in waves:
+        rs_next(j0, n, 3)
+    for i in range(CUTS):
+        rs_next(i * D, D, 4)
+    for j0 in (LOWER, UPPER):
+        rs_take(j0, CUTS, 3)
+        for i in range(CUTS):
+            rs_next(j0 + i, 1, 4, taken=True)
     outs = []
     for i in range(CUTS):
         rs_take(i * D, D, 4)
@@ -354,15 +360,17 @@
             fin_edge[i, h] = jnp.transpose(rs_sum(i * D, D, h), (1, 0, 2))
         lanes = pl.ds(pl.multiple_of(yl * HALF + i * LANE, LANE), LANE)
         outs += deliver(fin_edge.at[i], edge_out.at[:, :, lanes])
-    for j, (j0, dst) in enumerate((
-        (LOWER, lower_out.at[:, pl.ds(pl.multiple_of(yl * HALF, LANE), HALF)]), (UPPER, upper_out.at[yl])
-    )):
-        rs_take(j0, CUTS, 4)
-        for h in range(YN):
-            total = rs_sum(j0, CUTS, h)
-            for i in range(CUTS):
-                fin[j, h, :, i * LANE:(i + 1) * LANE] = total[i]
-        outs += deliver(fin.at[j], dst)
+    for j, j0 in enumerate((LOWER, UPPER)):
+        for i in range(CUTS):
+            rs_take(j0 + i, 1, 4)
+            cut = pl.ds(i * LANE, LANE)
+            for h in range(YN):
+                fin[j, h, :, cut] = rs_sum(j0 + i, 1, h)[0]
+            if j == 0:
+                dst = lower_out.at[:, pl.ds(pl.multiple_of(yl * HALF + i * LANE, LANE), LANE)]
+            else:
+                dst = upper_out.at[yl, :, cut]
+            outs += deliver(fin.at[j, :, :, cut], dst)
     rest = e2.at[pl.ds(1, ZN - 1)]
     pltpu.make_async_copy(rest, rest, asem.at[1]).wait()
 

time: 85.3 us -> 85.1 us (level)
  no operation moved by 1% of the time
where the time goes in v7:
time: 85.1 us; the launch traced here: 85 us
  Pallas kernels  84.3 us (99%)
    pallas_call x1, Pallas kernels, shards(): pl.pallas_call(kernel, out_shape=(jax.ShapeDtypeStruct((BLK, D, CHI), BF)...  82.6 us
    pallas_call x1, Pallas kernels, shards(): pl.pallas_call(settle, out_shape=(jax.ShapeDtypeStruct((BLK, D, CHI), BF)...  1.77 us

profile of v7, /device:TPU:1, one launch (start us, length us, event | category | flops | bytes accessed | tf_op | source)
XLA Modules:
  0.0 85.0 jit_solution(16668909123949453164)
XLA Ops:
  0.6 82.6 %shard_map.103 = (bf16[48,4,768]{2,1,0:T(4,128)(2,1)}, bf16[48,768]{1,0:T(8,128)(2,1)}, bf16[2,48,384]{2,1,0:T(8,128)(2,1)}) custom-call(bf16[48,4,768]{2,1,0:T(4,128)(2,1)} %bitcast.11, bf16[48,4,768]{2,1,0:T(4,128)(2,1)} %bitcast.12, bf16[48,4,768]{2,1,0:T(4,128)(2,1)} %bitcast.13, bf16[48,4,768]{2,1,0:T(4,128)(2,1)} %bitcast.14, ...), custom_call_target="tpu_custom_call" | custom-call | tf_op jit(solution)/shard_map/pallas_call | solution.py:414
  83.2 1.8 %shard_map.104 = (bf16[48,4,768]{2,1,0:T(4,128)(2,1)}, bf16[48,768]{1,0:T(8,128)(2,1)}, bf16[48,768]{1,0:T(8,128)(2,1)}) custom-call(bf16[48,4,768]{2,1,0:T(4,128)(2,1)} %get-tuple-element.9.edge_in, bf16[48,768]{1,0:T(8,128)(2,1)} %get-tuple-element.10.lower_in, bf16[2,48,384]{2,1,0:T(8,128)(2,1)} %get-tuple-element.11.upper_in), custom_call_target="tpu_custom_call" | custom-call | tf_op jit(solution)/shard_map/pallas_call | solution.py:462

commit v8 on v7

--- a/solution.py
+++ b/solution.py
@@ -73,13 +73,15 @@
 
     for source in sources:
         greet(source)
-    for half in range(YN):
-        for q in range(ZN // 2):
-            zz = yl * (ZN // 2) + q
-
-            @pl.when(half * ZN + zz != bond)
-            def _():
-                greet(at_bond(half, zz))
+    for k in range(ZN // 2):
+        zz = yl * (ZN // 2) + lax.rem(zq + k, ZN // 2)
+        greet(at_bond(yo, zz))
+        if k:
+            greet(at_bond(yl, zz))
+
+    @pl.when(zh != yl)
+    def _():
+        greet(at_bond(yl, yl * (ZN // 2) + zq))
 
     loads[0].wait()
     turned = jnp.transpose(pu[...], (1, 0, 2))

time: 85.1 us -> 85.1 us (level)
  no operation moved by 1% of the time
where the time goes in v8:
time: 85.1 us; the launch traced here: 85 us
  Pallas kernels  84.4 us (99%)
    pallas_call x1, Pallas kernels, shards(): pl.pallas_call(kernel, out_shape=(jax.ShapeDtypeStruct((BLK, D, CHI), BF)...  82.6 us
    pallas_call x1, Pallas kernels, shards(): pl.pallas_call(settle, out_shape=(jax.ShapeDtypeStruct((BLK, D, CHI), BF)...  1.77 us

profile of v8, /device:TPU:1, one launch (start us, length us, event | category | flops | bytes accessed | tf_op | source)
XLA Modules:
  0.0 85.0 jit_solution(14091175523128378009)
XLA Ops:
  0.6 82.6 %shard_map.103 = (bf16[48,4,768]{2,1,0:T(4,128)(2,1)}, bf16[48,768]{1,0:T(8,128)(2,1)}, bf16[2,48,384]{2,1,0:T(8,128)(2,1)}) custom-call(bf16[48,4,768]{2,1,0:T(4,128)(2,1)} %bitcast.11, bf16[48,4,768]{2,1,0:T(4,128)(2,1)} %bitcast.12, bf16[48,4,768]{2,1,0:T(4,128)(2,1)} %bitcast.13, bf16[48,4,768]{2,1,0:T(4,128)(2,1)} %bitcast.14, ...), custom_call_target="tpu_custom_call" | custom-call | tf_op jit(solution)/shard_map/pallas_call | solution.py:416
  83.2 1.8 %shard_map.104 = (bf16[48,4,768]{2,1,0:T(4,128)(2,1)}, bf16[48,768]{1,0:T(8,128)(2,1)}, bf16[48,768]{1,0:T(8,128)(2,1)}) custom-call(bf16[48,4,768]{2,1,0:T(4,128)(2,1)} %get-tuple-element.9.edge_in, bf16[48,768]{1,0:T(8,128)(2,1)} %get-tuple-element.10.lower_in, bf16[2,48,384]{2,1,0:T(8,128)(2,1)} %get-tuple-element.11.upper_in), custom_call_target="tpu_custom_call" | custom-call | tf_op jit(solution)/shard_map/pallas_call | solution.py:464

commit v9 on v8

--- a/solution.py
+++ b/solution.py
@@ -138,10 +138,10 @@
             if at is not None:
                 rcopy(at[0], at[1], to, ring[name, m])
 
+    y_pu = rcopy(put.at[yo], pu_at(yl, z), mate, fresh())
     loads[1].wait()
     both("cu", 1, (cu_at(z), cu_at(z)), (cu_at(z), cu_at(z)))
     both("own", 1, (put.at[yl], pu_at(yl, z)), (put.at[yl], pu_at(yl, z)))
-    y_pu = rcopy(put.at[yo], pu_at(yl, z), mate, fresh())
     keep = pltpu.make_async_copy(put.at[yl], pu_at(yl, z), lsem.at[8])
     keep.start()
     for load in loads[2:]:

time: 85.1 us -> 85.1 us (level)
  no operation moved by 1% of the time
where the time goes in v9:
time: 85.1 us; the launch traced here: 85 us
  Pallas kernels  84.4 us (99%)
    pallas_call x1, Pallas kernels, shards(): pl.pallas_call(kernel, out_shape=(jax.ShapeDtypeStruct((BLK, D, CHI), BF)...  82.6 us
    pallas_call x1, Pallas kernels, shards(): pl.pallas_call(settle, out_shape=(jax.ShapeDtypeStruct((BLK, D, CHI), BF)...  1.77 us

profile of v9, /device:TPU:1, one launch (start us, length us, event | category | flops | bytes accessed | tf_op | source)
XLA Modules:
  0.0 85.0 jit_solution(13751862214684255498)
XLA Ops:
  0.6 82.6 %shard_map.103 = (bf16[48,4,768]{2,1,0:T(4,128)(2,1)}, bf16[48,768]{1,0:T(8,128)(2,1)}, bf16[2,48,384]{2,1,0:T(8,128)(2,1)}) custom-call(bf16[48,4,768]{2,1,0:T(4,128)(2,1)} %bitcast.11, bf16[48,4,768]{2,1,0:T(4,128)(2,1)} %bitcast.12, bf16[48,4,768]{2,1,0:T(4,128)(2,1)} %bitcast.13, bf16[48,4,768]{2,1,0:T(4,128)(2,1)} %bitcast.14, ...), custom_call_target="tpu_custom_call" | custom-call | tf_op jit(solution)/shard_map/pallas_call | solution.py:416
  83.2 1.8 %shard_map.104 = (bf16[48,4,768]{2,1,0:T(4,128)(2,1)}, bf16[48,768]{1,0:T(8,128)(2,1)}, bf16[48,768]{1,0:T(8,128)(2,1)}) custom-call(bf16[48,4,768]{2,1,0:T(4,128)(2,1)} %get-tuple-element.9.edge_in, bf16[48,768]{1,0:T(8,128)(2,1)} %get-tuple-element.10.lower_in, bf16[2,48,384]{2,1,0:T(8,128)(2,1)} %get-tuple-element.11.upper_in), custom_call_target="tpu_custom_call" | custom-call | tf_op jit(solution)/shard_map/pallas_call | solution.py:464
